TPU v7x, 32 devices: a whole 2x2x4 slice. The times are simulated.
32 devices in a mesh: strip: 8 (over z, x), cells: 4 (over y, core).
Axes of the slice: x: 2, y: 2, z: 4, core: 2. Of those that a mesh axis runs over, the one named last changes fastest.
Arguments:
- pin_rows: int32 [131072], P(('strip', 'cells')), may hold values from 0 to 2
- pin_cols: int32 [131072], P(('strip', 'cells')), may hold values from 0 to 2558
- pin_fracs: float32 [2, 131072], P(None, ('strip', 'cells')), may hold values from 0 to 1
- pin_weights: float32 [131072], P(('strip', 'cells')), may hold values from 0.5 to 1.5
- capacity: int32 [32, 2560], P('strip', 'cells'), may hold values from 1 to 4
- blockage: float32 [32, 2560], P('strip', 'cells'), may hold values from 0 to 0.5
- row_blocks: float32 [20, 128, 128], P('cells'), may hold values from -0.002 to 0.15
- col_blocks: float32 [1, 32, 32], replicated, may hold values from -0.002 to 0.15
Outputs:
- final_density: float32 [32, 2560], P('strip', 'cells')
- pin_velocity: float32 [2, 131072], P(None, ('strip', 'cells'))
All inputs are finite; a program needn't handle non-finite values.
Results may differ from a plain program's by a relative error of at most 0.0052.
Values may be sent and summed in bfloat16 or wider, within the bound.
No kernel may reach another device: no remote copies, remote signals or barrier semaphores. Data moves between devices by JAX's collectives and lax.ppermute only.
A program may use at most 64 MiB of HBM per device.

v0:
```python
import functools

import jax
import jax.numpy as jnp
from jax import lax
from jax.experimental import pallas as pl
from jax.experimental.pallas import tpu as pltpu
from jax.sharding import PartitionSpec as P

SWEEPS = 3
STEPS = 2
LANES = 128
GROUP = 8

coupling = 2.0
floor_level = 0.5
block_low, block_span = -0.002, 0.152
weight_low, weight_span = 0.5, 3.5
term_low, term_octaves = -20.0, 34.0
code_top = 65535.0
code_half = 32768.0
log_two = 0.6931471805599453

f32 = jnp.float32
bf16 = jnp.bfloat16


def iota(shape, axis):
    return lax.broadcasted_iota(jnp.int32, shape, axis)


def halves(values):
    high = values.astype(bf16)
    return high, (values - high.astype(f32)).astype(bf16)


def last_dims(left, right):
    return lax.dot_general(left, right, (((1,), (1,)), ((), ())), preferred_element_type=f32)


def pick(index, first, near, far):
    return jnp.where(index == first, near, jnp.where(index == first + 1, far, 0.0))


def rounded(values):
    return values.astype(bf16).astype(f32)


def coded(share):
    return jnp.clip(jnp.round(share * code_top), 0.0, code_top) - code_half


def stored(codes):
    return codes.astype(jnp.int32).astype(jnp.int16)


def density_codes(values):
    octave = jnp.log(jnp.maximum(values, 2.0**-40)) * (1.0 / log_two)
    return stored(coded((octave - term_low) * (1.0 / term_octaves)))


def densities(codes):
    codes = codes.astype(f32)
    octave = (codes + code_half) * (term_octaves / code_top) + term_low
    return jnp.where(codes == -code_half, 0.0, jnp.exp(octave * log_two))


def splat_kernel(
    tiles, parts, rows_in, cols_in, fracs_in, pin_weights_in, row_blocks_in, cap_in, block_in, out_ref,
    rows_ref, cols_ref, fracs_ref, pin_weights_ref, row_blocks_ref, cap_ref, block_ref, arrived,
):
    depth = cap_ref.shape[0]
    height = parts * depth
    sources = (rows_in, cols_in, fracs_in, pin_weights_in, row_blocks_in, cap_in, block_in)
    places = (rows_ref, cols_ref, fracs_ref, pin_weights_ref, row_blocks_ref, cap_ref, block_ref)
    copies = [
        pltpu.make_async_copy(source, place, arrived.at[n]) for n, (source, place) in enumerate(zip(sources, places))
    ]
    for copy in copies:
        copy.start()
    for copy in copies[:4]:
        copy.wait()
    rows, cols, sizes = rows_ref[...], cols_ref[...], pin_weights_ref[...]
    place = iota((height * (tiles + 1), LANES), 0)
    group, inner = place // height, place % height
    keys = ((inner // depth) * tiles + group - 1) * depth + inner % depth
    lane = iota((LANES + 8, LANES), 0)
    tables, lanes = [], []
    for j in range(rows.shape[0]):
        cut = slice(j * LANES, (j + 1) * LANES)
        fy, fx = fracs_ref[0:1, cut], fracs_ref[1:2, cut]
        size, col = sizes[j : j + 1], cols[j : j + 1]
        key = (col >> 7) * depth + rows[j : j + 1]
        tables.append(pick(keys, key, rounded(size * (1.0 - fy)), rounded(size * fy)).astype(bf16))
        lanes.append(pick(lane, col & 127, rounded(1.0 - fx), rounded(fx)).astype(bf16))
    total = last_dims(jnp.concatenate(tables, 1), jnp.concatenate(lanes, 1))
    for copy in copies[4:]:
        copy.wait()
    first_lane = iota((height, LANES), 1) == 0
    for t in range(tiles):
        own = total[(t + 1) * height : (t + 2) * height, :LANES]
        spill = total[t * height : (t + 1) * height, LANES : LANES + 1]
        own = own + jnp.where(first_lane, spill, 0.0)
        cut = slice(t * LANES, (t + 1) * LANES)
        out_ref[:height, cut] = density_codes(own)
        share = (row_blocks_ref[t * LANES : (t + 1) * LANES, :] - block_low) * (1.0 / block_span)
        out_ref[2 * height :, cut] = stored(coded(share))
    weights = cap_ref[...].astype(f32) * (1.0 - block_ref[...])
    code = coded((weights - weight_low) * (1.0 / weight_span))
    row = iota((height, weights.shape[1]), 0)
    mine = row // depth == lax.axis_index("cells")
    out_ref[height : 2 * height, :] = stored(jnp.where(mine, jnp.concatenate([code] * parts, 0), 0.0))


def sum_kernel(*refs):
    sent_refs, out_ref = refs[:-1], refs[-1]
    height = out_ref.shape[0] // 2
    terms, codes = 0.0, 0.0
    for sent_ref in sent_refs:
        terms += densities(sent_ref[:height, :])
        codes += sent_ref[height:, :].astype(f32)
    out_ref[:height, :] = density_codes(terms)
    out_ref[height:, :] = stored(codes)


def beside(values):
    width = values.shape[1]
    lane = iota((values.shape[0], LANES), 1)
    left, right = pltpu.roll(values, 1, 1), pltpu.roll(values, width - 1, 1)
    first = jnp.where(lane == 0, values[:, :LANES], left[:, :LANES])
    last = jnp.where(lane == LANES - 1, values[:, width - LANES :], right[:, width - LANES :])
    return (
        jnp.concatenate([first, left[:, LANES:]], 1),
        jnp.concatenate([right[:, : width - LANES], last], 1),
    )


class Turned:
    def __init__(self, tiles):
        self.tiles, self.turned = tiles, {}

    def turn(self, t, shift):
        if (t, shift) not in self.turned:
            self.turned[t, shift] = pltpu.roll(self.tiles[t], shift, 1)
        return self.turned[t, shift]

    def along(self, t):
        mine, back = self.tiles[t], LANES - 1
        lane = iota(mine.shape, 1)
        before = self.turn(t - 1, 1) if t else mine
        after = self.turn(t + 1, back) if t + 1 < len(self.tiles) else mine
        left = jnp.where(lane == 0, before, self.turn(t, 1))
        right = jnp.where(lane == back, after, self.turn(t, back))
        return 2.0 * mine - left - right


def delayed(count, first, second, delay=2):
    waiting, results = [], []
    for t in range(count + delay):
        if t < count:
            waiting.append(first(t))
        if t >= delay:
            results.append(second(t - delay, waiting[t - delay]))
            waiting[t - delay] = None
    return results


def across_lines(values):
    height = values.shape[0]
    row = iota((8, values.shape[1]), 0)
    above, below = pltpu.roll(values, 1, 0), pltpu.roll(values, height - 1, 0)
    first = jnp.where(row == 0, values[:8], above[:8])
    last = jnp.where(row == 7, values[height - 8 :], below[height - 8 :])
    above = jnp.concatenate([first, above[8:]], 0)
    below = jnp.concatenate([below[: height - 8], last], 0)
    return 2.0 * values - above - below


def col_products(residual, blocks):
    high, low = halves(residual)
    size = blocks[0].shape[0] // 2
    dot = functools.partial(jnp.dot, preferred_element_type=f32)
    cuts = [slice(k * size, (k + 1) * size) for k in range(len(blocks))]
    return [(dot(pair, high[cut]), dot(pair[:size], low[cut])) for pair, cut in zip(blocks, cuts)]


def col_sum(products):
    size = products[0][1].shape[0]
    result = [both[:size] + (both[size:] + rest) for both, rest in products]
    return result[0] if len(result) == 1 else jnp.concatenate(result, 0)


def each(count, body):
    if count == 1:
        body(0)
    else:
        pl.loop(0, count)(body)


def join_kernel(*refs):
    for n, ref in enumerate(refs[:-1]):
        refs[-1][n * ref.shape[0] : (n + 1) * ref.shape[0], :] = ref[...]


def unpack_kernel(tiles, carried, codes_ref, pairs_ref):
    for k in range(pairs_ref.shape[0]):
        base = (k // tiles) * (carried + LANES) + carried
        code = codes_ref[base : base + LANES, k % tiles * LANES : (k % tiles + 1) * LANES].astype(f32)
        high, low = halves((code + code_half) * (block_span / code_top) + block_low)
        pairs_ref[k, :LANES, :] = high
        pairs_ref[k, LANES:, :] = low


def field_kernel(
    sizes, pairs, col_blocks_ref, rows_ref, cols_ref, fracs_ref, *refs,
):
    depth, tiles, parts, strips = sizes
    sent_refs, (final_ref, velocity_ref, weights_ref, source_ref, field_ref, ordered) = refs[:-6], refs[-6:]
    width_part = tiles * LANES
    width = parts * width_part
    height = strips * depth
    chunk = min(GROUP, strips) * depth
    chunks = height // chunk
    strip, part = lax.axis_index("strip"), lax.axis_index("cells")

    slots = parts * depth
    if len(sent_refs) == 1:
        sent = sent_refs[0]
    else:
        sent = ordered
        for near, sent_ref in enumerate(sent_refs):
            for n in range(strips // 2):
                ordered[strip ^ (2 * n + near)] = sent_ref[n * 2 * slots : (n + 1) * 2 * slots, :]
    group = chunk // depth
    target, origin = iota((parts * chunk, group * slots), 0), iota((parts * chunk, group * slots), 1)
    slot = origin % slots
    fits = (slot // depth == target // chunk) & (origin // slots * depth + slot % depth == target % chunk)
    chosen = jnp.where(fits, 1.0, 0.0).astype(bf16)

    def placed(values):
        high, low = halves(jnp.concatenate(values, 0))
        dot = functools.partial(jnp.dot, preferred_element_type=f32)
        return dot(chosen, high) + dot(chosen, low)

    @functools.partial(each, chunks)
    def place(g):
        terms, codes = [], []
        for n in range(group):
            got = sent[g * group + n]
            terms.append(densities(got[:slots]))
            codes.append(got[slots:].astype(f32))
        term = placed(terms)
        weight = (placed(codes) + code_half) * (weight_span / code_top) + weight_low
        here = pl.ds(pl.multiple_of(g * chunk, chunk), chunk)
        for p in range(parts):
            cut = slice(p * width_part, (p + 1) * width_part)
            weights_ref[here, cut] = weight[p * chunk : (p + 1) * chunk]
            source_ref[here, cut] = term[p * chunk : (p + 1) * chunk] / weight[p * chunk : (p + 1) * chunk]

    col_blocks = [jnp.concatenate(halves(col_blocks_ref[k]), 0) for k in range(col_blocks_ref.shape[0])]
    inner = pl.ds(8, height)
    lanes_at_once = 2 * LANES if chunks == 1 and width % (2 * LANES) == 0 else LANES
    at_once = width // lanes_at_once if chunks == 1 else 1

    def cuts_of(g):
        if at_once > 1:
            return [slice(n * lanes_at_once, (n + 1) * lanes_at_once) for n in range(at_once)]
        return [pl.ds(pl.multiple_of(g * lanes_at_once, lanes_at_once), lanes_at_once)]

    col_steps = width // lanes_at_once // at_once

    @functools.partial(each, col_steps)
    def start(g):
        for cut in cuts_of(g):
            current = source_ref[:, cut]
            field_ref[inner, cut] = current
            source_ref[:, cut] = weights_ref[:, cut] * current - coupling * across_lines(current)

    row_tiles = [slice(t * LANES, (t + 1) * LANES) for t in range(width // LANES)]
    for step in range(STEPS):

        @functools.partial(each, chunks)
        def solve_rows(g):
            here = pl.ds(pl.multiple_of(g * chunk, chunk), chunk)
            there = pl.ds(pl.multiple_of(g * chunk + 8, 8), chunk)
            current = [field_ref[there, cut] for cut in row_tiles]
            for sweep in range(SWEEPS):
                turned = Turned(current)

                def multiply(t):
                    cut = row_tiles[t]
                    now = weights_ref[here, cut] * turned.tiles[t] + coupling * turned.along(t)
                    return last_dims(jnp.concatenate(halves(source_ref[here, cut] - now), 0), pairs[t])

                def add(t, product):
                    high, low = product[:chunk], product[chunk:]
                    return turned.tiles[t] + (high[:, :LANES] + (high[:, LANES:] + low[:, :LANES]))

                current = delayed(len(current), multiply, add)
            turned = Turned(current)
            for t, cut in enumerate(row_tiles):
                field_ref[there, cut] = current[t]
                source_ref[here, cut] = weights_ref[here, cut] * current[t] - coupling * turned.along(t)

        @functools.partial(each, col_steps)
        def solve_cols(g):
            cuts = cuts_of(g)
            current = [field_ref[inner, cut] for cut in cuts]
            for sweep in range(SWEEPS):
                before = current

                def multiply(n):
                    now = weights_ref[:, cuts[n]] * before[n] + coupling * across_lines(before[n])
                    return col_products(source_ref[:, cuts[n]] - now, col_blocks)

                current = delayed(len(cuts), multiply, lambda n, products: before[n] + col_sum(products))
            for now, cut in zip(current, cuts):
                field_ref[inner, cut] = now
                if step + 1 < STEPS:
                    source_ref[:, cut] = weights_ref[:, cut] * now - coupling * across_lines(now)
                else:
                    field_ref[:8, cut] = jnp.broadcast_to(now[:1], (8, lanes_at_once))
                    field_ref[height + 8 :, cut] = jnp.broadcast_to(now[-1:], (8, lanes_at_once))

    row0 = strip * depth
    columns = pl.ds(pl.multiple_of(part * width_part, LANES), width_part)
    base, shift = pl.multiple_of(row0 // 8 * 8, 8), 17 - row0 % 8
    final_ref[...] = pltpu.roll(field_ref[pl.ds(base, 24), columns], shift, 0)[1 : 1 + depth]

    window = pltpu.roll(field_ref[pl.ds(base, 24), :], shift, 0)
    above, centre, below = window[:8], pltpu.roll(window, 23, 0)[:8], pltpu.roll(window, 22, 0)[:8]
    left, right = beside(centre)
    scale = jnp.maximum(centre, floor_level)
    velocity_y = rounded(-(0.5 * (below - above)) / scale)
    velocity_x = rounded(-(0.5 * (right - left)) / scale)

    upper = iota((8, LANES), 0) < depth

    def stacked(values):
        stack = []
        for t in range(0, parts * tiles, 2):
            even = values[:, t * LANES : (t + 1) * LANES]
            odd = values[:, (t + 1) * LANES : (t + 2) * LANES]
            stack.append(jnp.where(upper, even, pltpu.roll(odd, depth, 0)))
        return jnp.concatenate(stack, 0)

    half = LANES // 2

    def table_of(values):
        stack = stacked(values)
        many = stack.shape[0]
        blank = jnp.zeros((LANES - many, LANES), f32)
        turned = jnp.concatenate([stack, blank], 0).T
        after = jnp.concatenate([pltpu.roll(stack, many - depth, 0), blank], 0).T[:8]
        return jnp.concatenate([turned[: half + 8], jnp.concatenate([turned[half:], after], 0)], 1)

    table = jnp.concatenate([table_of(velocity_y), table_of(velocity_x)], 0).astype(bf16)
    many = parts * tiles * depth
    rows, cols = rows_ref[...], cols_ref[...]
    joined = 2 if rows.shape[0] % 2 == 0 else 1
    blank = jnp.zeros((LANES - many, joined * LANES), bf16)
    keys, lane = iota((many, joined * LANES), 0), iota((half + 8, joined * LANES), 0)
    for j in range(0, rows.shape[0], joined):
        cut = slice(j * LANES, (j + joined) * LANES)
        fy, fx = fracs_ref[0:1, cut], fracs_ref[1:2, cut]
        col = jnp.concatenate([cols[n : n + 1] for n in range(j, j + joined)], 1)
        row = jnp.concatenate([rows[n : n + 1] for n in range(j, j + joined)], 1)
        key = (col >> 7) * depth + row
        second = (col & half) != 0
        near, far = rounded(1.0 - fy), rounded(fy)
        looks = [
            pick(keys, jnp.where(second, -8, key), near, far).astype(bf16),
            blank,
            pick(keys, jnp.where(second, key, -8), near, far).astype(bf16),
            blank,
        ]
        sampled = jnp.dot(table, jnp.concatenate(looks, 0), preferred_element_type=f32)
        share = pick(lane, col & (half - 1), rounded(1.0 - fx), rounded(fx))
        velocity_ref[0:1, cut] = jnp.sum(sampled[: half + 8] * share, 0, keepdims=True)
        velocity_ref[1:2, cut] = jnp.sum(sampled[half + 8 :] * share, 0, keepdims=True)


def partner(values, axis, bits):
    return lax.ppermute(values, axis, [(n, n ^ bits) for n in range(lax.axis_size(axis))])


def local(pin_rows, pin_cols, pin_fracs, pin_weights, capacity, blockage, row_blocks, col_blocks):
    depth, width_part = capacity.shape
    parts, strips = lax.axis_size("cells"), lax.axis_size("strip")
    tiles = width_part // LANES
    height, width = depth * strips, width_part * parts
    pins = pin_rows.shape[0]
    by_lane = (pins // LANES, LANES)
    rows, cols = pin_rows.reshape(by_lane), pin_cols.reshape(by_lane)
    sizes = pin_weights.reshape(by_lane)
    vmem = pl.BlockSpec(memory_space=pltpu.VMEM)
    whole = pltpu.CompilerParams(vmem_limit_bytes=60 << 20)
    small = pltpu.CompilerParams(vmem_limit_bytes=16 * 1024 * 1024)
    grid_bytes = 4 * height * width
    large = pltpu.CompilerParams(vmem_limit_bytes=(20 << 20) + 6 * grid_bytes)

    carried = 2 * parts * depth
    read = (rows, cols, pin_fracs, sizes, row_blocks.reshape(-1, LANES), capacity, blockage)
    terms = pl.pallas_call(
        functools.partial(splat_kernel, tiles, parts),
        out_shape=jax.ShapeDtypeStruct((carried + LANES, width_part), jnp.int16),
        in_specs=[pl.BlockSpec(memory_space=pltpu.HBM)] * 7,
        out_specs=vmem,
        scratch_shapes=[pltpu.VMEM(item.shape, item.dtype) for item in read] + [pltpu.SemaphoreType.DMA((7,))],
        compiler_params=whole,
        name="splat",
    )(*read)
    blocks = lax.all_gather(terms, "cells", axis=0, tiled=True)

    def terms_of(part):
        place = part * (carried + LANES) // carried
        return pl.BlockSpec((carried, width_part), lambda i: (place, 0))

    sums = pl.pallas_call(
        sum_kernel,
        grid=(1,),
        out_shape=jax.ShapeDtypeStruct((carried, width_part), jnp.int16),
        in_specs=[terms_of(part) for part in range(parts)],
        out_specs=pl.BlockSpec((carried, width_part), lambda i: (0, 0)),
        compiler_params=small,
        name="sum_terms",
    )(*[blocks] * parts)
    if strips == 8:
        from_z = {k: partner(sums, "strip", k) for k in (6, 4, 2)}
        held = pl.pallas_call(
            join_kernel,
            out_shape=jax.ShapeDtypeStruct((strips // 2 * carried, width_part), jnp.int16),
            in_specs=[vmem] * 4,
            out_specs=vmem,
            compiler_params=small,
            name="join",
        )(sums, from_z[2], from_z[4], from_z[6])
        held, blocks = lax.optimization_barrier((held, blocks))
        sent = [held, partner(held, "strip", 1)]
    else:
        sent = [lax.all_gather(sums, "strip", axis=0)]
    pairs = pl.pallas_call(
        functools.partial(unpack_kernel, tiles, carried),
        out_shape=jax.ShapeDtypeStruct((width // LANES, 2 * LANES, LANES), bf16),
        in_specs=[vmem],
        out_specs=vmem,
        compiler_params=small,
        cost_estimate=pl.CostEstimate(flops=1 << 20, bytes_accessed=1 << 21, transcendentals=0),
        name="unpack",
    )(blocks)

    final, velocity = pl.pallas_call(
        functools.partial(field_kernel, (depth, tiles, parts, strips)),
        out_shape=(
            jax.ShapeDtypeStruct((depth, width_part), f32),
            jax.ShapeDtypeStruct((2, pins), f32),
        ),
        in_specs=[vmem] * (5 + len(sent)),
        out_specs=(vmem, vmem),
        scratch_shapes=[
            pltpu.VMEM((height, width), f32),
            pltpu.VMEM((height, width), f32),
            pltpu.VMEM((height + 16, width), f32),
            pltpu.VMEM((strips if len(sent) > 1 else 1, carried, width_part), jnp.int16),
        ],
        compiler_params=large,
        name="field",
    )(pairs, col_blocks, rows, cols, pin_fracs, *sent)
    return final, velocity


def solution(mesh):
    placed = (
        P(("strip", "cells")),
        P(("strip", "cells")),
        P(None, ("strip", "cells")),
        P(("strip", "cells")),
        P("strip", "cells"),
        P("strip", "cells"),
        P("cells", None, None),
        P(),
    )
    return jax.shard_map(
        local,
        mesh=mesh,
        in_specs=placed,
        out_specs=(P("strip", "cells"), P(None, ("strip", "cells"))),
        check_vma=False,
    )
```

profile of v0, /device:TPU:0, one launch (start us, length us, event | category | flops | bytes accessed | tf_op | source)
XLA Modules:
  0.0 35.8 jit_solution(16725677973984502874)
XLA Ops:
  0.6 2.6 %splat.1 = s16[160,640]{1,0:T(8,128)(2,1)} custom-call(s32[32,128]{1,0:T(8,128)} %bitcast.4, s32[32,128]{1,0:T(8,128)} %bitcast.6, f32[2,4096]{1,0:T(2,128)} %fracs_ref.1, f32[32,128]{1,0:T(8,128)} %bitcast.9, f32[640,128]{1,0:T(8,128)} %bitcast.8, s32[4,640]{1,0:T(4,128)} %cap_in.1, f32[4,640]{1,0:T(4,128)} %block_in.1), custom_call_target="tpu_custom_call" | custom-call | tf_op jit(solution)/shard_map/splat/pallas_call | solution.py:404
  3.3 10.5 %all_gather.3.refs_0_.refs_1_.refs_2_.refs_3_.codes_ref = s16[640,640]{1,0:T(8,128)(2,1)S(1)} all-gather(s16[160,640]{1,0:T(8,128)(2,1)} %splat.1), channel_id=1, replica_groups=mesh['strip'=8,'cells'=4] {'cells'}, dimensions={0}, use_global_device_ids=true | all-gather | bytes 1024000 | tf_op jit(solution)/shard_map/all_gather | solution.py:413
  13.7 0.1 sum_terms.1.refs_0_
  13.8 0.0 copy-start
  13.8 0.0 copy-start.1
  13.9 0.0 copy-start.2
  13.9 0.0 copy-start.3
  13.9 1.6 %collective-permute-start = (s16[32,640]{1,0:T(8,128)(2,1)S(1)}, s16[32,640]{1,0:T(8,128)(2,1)S(1)}, u32[]{:S(2)}, u32[]{:S(2)}) collective-permute-start(s16[32,640]{1,0:T(8,128)(2,1)S(1)} %sum_terms.1.refs_0_), channel_id=1, source_target_pairs={{0,8},{4,12},{8,0},{12,4},{16,24},{20,28},{24,16},{28,20},{1,9},{5... | collective-permute-start | bytes 122888 | tf_op jit(solution)/shard_map/ppermute | solution.py:384
  15.5 2.6 %collective-permute-start.1 = (s16[32,640]{1,0:T(8,128)(2,1)S(1)}, s16[32,640]{1,0:T(8,128)(2,1)S(1)}, u32[]{:S(2)}, u32[]{:S(2)}) collective-permute-start(s16[32,640]{1,0:T(8,128)(2,1)S(1)} %sum_terms.1.refs_0_), channel_id=1, source_target_pairs={{0,16},{4,20},{8,24},{12,28},{16,0},{20,4},{24,8},{28,12},{1,17},{... | collective-permute-start | bytes 122888 | tf_op jit(solution)/shard_map/ppermute | solution.py:384
  18.1 0.2 collective-permute-start.2
  18.3 0.0 collective-permute-done.refs_1_
  18.3 2.8 %collective-permute-done.1.refs_2_ = s16[32,640]{1,0:T(8,128)(2,1)S(1)} collective-permute-done((s16[32,640]{1,0:T(8,128)(2,1)S(1)}, s16[32,640]{1,0:T(8,128)(2,1)S(1)}, u32[]{:S(2)}, u32[]{:S(2)}) %collective-permute-start.1) | collective-permute-done | bytes 40992 | tf_op jit(solution)/shard_map/ppermute | solution.py:384
  21.2 2.7 %collective-permute-done.2.refs_3_ = s16[32,640]{1,0:T(8,128)(2,1)S(1)} collective-permute-done((s16[32,640]{1,0:T(8,128)(2,1)S(1)}, s16[32,640]{1,0:T(8,128)(2,1)S(1)}, u32[]{:S(2)}, u32[]{:S(2)}) %collective-permute-start.2) | collective-permute-done | bytes 40992 | tf_op jit(solution)/shard_map/ppermute | solution.py:384
  23.9 1.6 %collective-permute-start.3 = (s16[128,640]{1,0:T(8,128)(2,1)S(1)}, s16[128,640]{1,0:T(8,128)(2,1)S(1)}, u32[]{:S(2)}, u32[]{:S(2)}) collective-permute-start(s16[128,640]{1,0:T(8,128)(2,1)S(1)} %join.1.refs_0_), channel_id=1, source_target_pairs={{0,4},{4,0},{8,12},{12,8},{16,20},{20,16},{24,28},{28,24},{1,5},{5... | collective-permute-start | bytes 491528 | tf_op jit(solution)/shard_map/ppermute | solution.py:384
  25.5 0.3 unpack.1.pairs
  25.8 3.5 %collective-permute-done.3.refs_1_ = s16[128,640]{1,0:T(8,128)(2,1)S(1)} collective-permute-done((s16[128,640]{1,0:T(8,128)(2,1)S(1)}, s16[128,640]{1,0:T(8,128)(2,1)S(1)}, u32[]{:S(2)}, u32[]{:S(2)}) %collective-permute-start.3) | collective-permute-done | bytes 163872 | tf_op jit(solution)/shard_map/ppermute | solution.py:384
  29.3 0.0 copy-done
  29.3 0.0 copy-done.1
  29.3 0.0 copy-done.2
  29.3 0.0 copy-done.3
  29.3 6.4 %field.1 = (f32[4,640]{1,0:T(4,128)}, f32[2,4096]{1,0:T(2,128)}) custom-call(bf16[20,256,128]{2,1,0:T(8,128)(2,1)S(1)} %unpack.1.pairs, f32[1,32,32]{2,1,0:T(8,128)S(1)} %copy-done.3, s32[32,128]{1,0:T(8,128)S(1)} %bitcast.5, s32[32,128]{1,0:T(8,128)S(1)} %bitcast.7, f32[2,4096]{1,0:T(2,128)S(1)} %copy-done, s16[128,640]{1,0:T(8,128)(2,1)S(1)} %join.1.refs_0_, ...), custom_call_target="tpu_custom_call" | custom-call | tf_op jit(solution)/shard_map/field/pallas_call | solution.py:452
  (1 shorter events, 0.0 us)
Async XLA Ops:
  13.8 15.5 %copy-start = (f32[2,4096]{1,0:T(2,128)S(1)}, f32[2,4096]{1,0:T(2,128)}, u32[]{:S(2)}) copy-start(f32[2,4096]{1,0:T(2,128)} %fracs_ref.1) | copy-start | bytes 98308
  13.8 15.5 %copy-start.1 = (s32[4096]{0:T(1024)S(1)}, s32[4096]{0:T(1024)}, u32[]{:S(2)}) copy-start(s32[4096]{0:T(1024)} %param.8) | copy-start | bytes 49156
  13.9 15.5 %copy-start.2 = (s32[4096]{0:T(1024)S(1)}, s32[4096]{0:T(1024)}, u32[]{:S(2)}) copy-start(s32[4096]{0:T(1024)} %param.9) | copy-start | bytes 49156
  13.9 15.5 %copy-start.3 = (f32[1,32,32]{2,1,0:T(8,128)S(1)}, f32[1,32,32]{2,1,0:T(8,128)}, u32[]{:S(2)}) copy-start(f32[1,32,32]{2,1,0:T(8,128)} %col_blocks_ref.1) | copy-start | bytes 12292
  13.9 4.5 %collective-permute-start = (s16[32,640]{1,0:T(8,128)(2,1)S(1)}, s16[32,640]{1,0:T(8,128)(2,1)S(1)}, u32[]{:S(2)}, u32[]{:S(2)}) collective-permute-start(s16[32,640]{1,0:T(8,128)(2,1)S(1)} %sum_terms.1.refs_0_), channel_id=1, source_target_pairs={{0,8},{4,12},{8,0},{12,4},{16,24},{20,28},{24,16},{28,20},{1,9},{5... | collective-permute-start | bytes 122888 | tf_op jit(solution)/shard_map/ppermute | solution.py:384
  15.5 5.7 %collective-permute-start.1 = (s16[32,640]{1,0:T(8,128)(2,1)S(1)}, s16[32,640]{1,0:T(8,128)(2,1)S(1)}, u32[]{:S(2)}, u32[]{:S(2)}) collective-permute-start(s16[32,640]{1,0:T(8,128)(2,1)S(1)} %sum_terms.1.refs_0_), channel_id=1, source_target_pairs={{0,16},{4,20},{8,24},{12,28},{16,0},{20,4},{24,8},{28,12},{1,17},{... | collective-permute-start | bytes 122888 | tf_op jit(solution)/shard_map/ppermute | solution.py:384
  18.1 5.8 %collective-permute-start.2 = (s16[32,640]{1,0:T(8,128)(2,1)S(1)}, s16[32,640]{1,0:T(8,128)(2,1)S(1)}, u32[]{:S(2)}, u32[]{:S(2)}) collective-permute-start(s16[32,640]{1,0:T(8,128)(2,1)S(1)} %sum_terms.1.refs_0_), channel_id=1, source_target_pairs={{0,24},{4,28},{8,16},{12,20},{16,8},{20,12},{24,0},{28,4},{1,25},{... | collective-permute-start | bytes 122888 | tf_op jit(solution)/shard_map/ppermute | solution.py:384
  23.9 5.4 %collective-permute-start.3 = (s16[128,640]{1,0:T(8,128)(2,1)S(1)}, s16[128,640]{1,0:T(8,128)(2,1)S(1)}, u32[]{:S(2)}, u32[]{:S(2)}) collective-permute-start(s16[128,640]{1,0:T(8,128)(2,1)S(1)} %join.1.refs_0_), channel_id=1, source_target_pairs={{0,4},{4,0},{8,12},{12,8},{16,20},{20,16},{24,28},{28,24},{1,5},{5... | collective-permute-start | bytes 491528 | tf_op jit(solution)/shard_map/ppermute | solution.py:384
where the time goes:
time: 36 us; the launch traced here: 35.8 us
  blocking collectives  10.5 us (29%)
  Pallas kernels  9.51 us (26%)
  waiting for transfers between devices  9.06 us (25%)
  starting transfers between devices  6.01 us (17%)
  between operations  0.7 us (2%)
    all_gather x1, blocking collectives, local(): blocks = lax.all_gather(terms, 'cells', axis=0, tiled=True)  10.5 us
    ppermute x4, waiting for transfers between devices, partner(): lax.ppermute(values, axis, [(n, n ^ bits) for n in range(lax.axis_size(ax...  9.06 us
    pallas_call x1, Pallas kernels, local(): pl.pallas_call(functools.partial(field_kernel, (depth, tiles, parts, stri...  6.43 us
    ppermute x4, starting transfers between devices, partner(): lax.ppermute(values, axis, [(n, n ^ bits) for n in range(lax.axis_size(ax...  6.01 us
    pallas_call x1, Pallas kernels, local(): pl.pallas_call(functools.partial(splat_kernel, tiles, parts), out_shape=j...  2.63 us
  transfers between devices with their start and end apart: 4, of which 3 were waited for; matrix products, arithmetic and copies ran while one was open for 0% of the time, Pallas kernels for 1%

commit v1 on v0

--- a/solution.py
+++ b/solution.py
@@ -56,7 +56,7 @@
 
 def density_codes(values):
     octave = jnp.log(jnp.maximum(values, 2.0**-40)) * (1.0 / log_two)
-    return stored(coded((octave - term_low) * (1.0 / term_octaves)))
+    return coded((octave - term_low) * (1.0 / term_octaves))
 
 
 def densities(codes):
@@ -102,7 +102,7 @@
         spill = total[t * height : (t + 1) * height, LANES : LANES + 1]
         own = own + jnp.where(first_lane, spill, 0.0)
         cut = slice(t * LANES, (t + 1) * LANES)
-        out_ref[:height, cut] = density_codes(own)
+        out_ref[:height, cut] = stored(density_codes(own))
         share = (row_blocks_ref[t * LANES : (t + 1) * LANES, :] - block_low) * (1.0 / block_span)
         out_ref[2 * height :, cut] = stored(coded(share))
     weights = cap_ref[...].astype(f32) * (1.0 - block_ref[...])
@@ -114,13 +114,16 @@
 
 def sum_kernel(*refs):
     sent_refs, out_ref = refs[:-1], refs[-1]
-    height = out_ref.shape[0] // 2
+    height = sent_refs[0].shape[0] // 2
     terms, codes = 0.0, 0.0
     for sent_ref in sent_refs:
         terms += densities(sent_ref[:height, :])
         codes += sent_ref[height:, :].astype(f32)
-    out_ref[:height, :] = density_codes(terms)
-    out_ref[height:, :] = stored(codes)
+    if out_ref.shape[0] == height:
+        out_ref[...] = stored(jnp.where(lax.axis_index("cells") % 2 == 0, density_codes(terms), codes))
+    else:
+        out_ref[:height, :] = stored(density_codes(terms))
+        out_ref[height:, :] = stored(codes)
 
 
 def beside(values):
@@ -226,11 +229,20 @@
     slots = parts * depth
     if len(sent_refs) == 1:
         sent = sent_refs[0]
+
+        def half_of(n, side):
+            return sent[n][side * slots : (side + 1) * slots]
+
     else:
-        sent = ordered
-        for near, sent_ref in enumerate(sent_refs):
-            for n in range(strips // 2):
-                ordered[strip ^ (2 * n + near)] = sent_ref[n * 2 * slots : (n + 1) * 2 * slots, :]
+        for other, sent_ref in enumerate(sent_refs):
+            for n in range(strips):
+                near, far = n // (strips // 2), n % (strips // 2)
+                got = sent_ref[n * slots : (n + 1) * slots, :]
+                ordered[strip ^ (2 * far + near), (part + other) % 2] = got
+
+        def half_of(n, side):
+            return ordered[n, side]
+
     group = chunk // depth
     target, origin = iota((parts * chunk, group * slots), 0), iota((parts * chunk, group * slots), 1)
     slot = origin % slots
@@ -246,9 +258,8 @@
     def place(g):
         terms, codes = [], []
         for n in range(group):
-            got = sent[g * group + n]
-            terms.append(densities(got[:slots]))
-            codes.append(got[slots:].astype(f32))
+            terms.append(densities(half_of(g * group + n, 0)))
+            codes.append(half_of(g * group + n, 1).astype(f32))
         term = placed(terms)
         weight = (placed(codes) + code_half) * (weight_span / code_top) + weight_low
         here = pl.ds(pl.multiple_of(g * chunk, chunk), chunk)
@@ -416,27 +427,34 @@
         place = part * (carried + LANES) // carried
         return pl.BlockSpec((carried, width_part), lambda i: (place, 0))
 
+    split = strips == 8 and parts % 2 == 0
+    handed = carried // 2 if split else carried
     sums = pl.pallas_call(
         sum_kernel,
         grid=(1,),
-        out_shape=jax.ShapeDtypeStruct((carried, width_part), jnp.int16),
+        out_shape=jax.ShapeDtypeStruct((handed, width_part), jnp.int16),
         in_specs=[terms_of(part) for part in range(parts)],
-        out_specs=pl.BlockSpec((carried, width_part), lambda i: (0, 0)),
+        out_specs=pl.BlockSpec((handed, width_part), lambda i: (0, 0)),
         compiler_params=small,
         name="sum_terms",
     )(*[blocks] * parts)
-    if strips == 8:
+    if split:
+
+        def joined(*items):
+            return pl.pallas_call(
+                join_kernel,
+                out_shape=jax.ShapeDtypeStruct((len(items) * items[0].shape[0], width_part), jnp.int16),
+                in_specs=[vmem] * len(items),
+                out_specs=vmem,
+                compiler_params=small,
+                name="join",
+            )(*items)
+
         from_z = {k: partner(sums, "strip", k) for k in (6, 4, 2)}
-        held = pl.pallas_call(
-            join_kernel,
-            out_shape=jax.ShapeDtypeStruct((strips // 2 * carried, width_part), jnp.int16),
-            in_specs=[vmem] * 4,
-            out_specs=vmem,
-            compiler_params=small,
-            name="join",
-        )(sums, from_z[2], from_z[4], from_z[6])
+        held = joined(sums, from_z[2], from_z[4], from_z[6])
         held, blocks = lax.optimization_barrier((held, blocks))
-        sent = [held, partner(held, "strip", 1)]
+        held = joined(held, partner(held, "strip", 1))
+        sent = [held, partner(held, "cells", 1)]
     else:
         sent = [lax.all_gather(sums, "strip", axis=0)]
     pairs = pl.pallas_call(
@@ -461,7 +479,7 @@
             pltpu.VMEM((height, width), f32),
             pltpu.VMEM((height, width), f32),
             pltpu.VMEM((height + 16, width), f32),
-            pltpu.VMEM((strips if len(sent) > 1 else 1, carried, width_part), jnp.int16),
+            pltpu.VMEM((strips if split else 1, 2, carried // 2, width_part), jnp.int16),
         ],
         compiler_params=large,
         name="field",

time: 36 us -> 36.4 us (1.011)
    ppermute x4 -> x5, waiting for transfers between devices: 9.06 us -> 9.34 us  [partner(): lax.ppermute(values, axis, [(n, n ^ bits) for n in range(lax.axis_size(ax...]
    ppermute x4 -> x5, starting transfers between devices: 6.01 us -> 6.08 us  [partner(): lax.ppermute(values, axis, [(n, n ^ bits) for n in range(lax.axis_size(ax...]
  transfers between devices with their start and end apart: 4 -> 5, of which waited for: 3 -> 4; matrix products, arithmetic and copies ran while one was open for 0% -> 0% of each run, Pallas kernels for 1% -> 1%
where the time goes in v1:
time: 36.4 us; the launch traced here: 36.1 us
  blocking collectives  10.5 us (29%)
  Pallas kernels  9.53 us (26%)
  waiting for transfers between devices  9.34 us (26%)
  starting transfers between devices  6.08 us (17%)
  between operations  0.71 us (2%)
    all_gather x1, blocking collectives, local(): blocks = lax.all_gather(terms, 'cells', axis=0, tiled=True)  10.5 us
    ppermute x5, waiting for transfers between devices, partner(): lax.ppermute(values, axis, [(n, n ^ bits) for n in range(lax.axis_size(ax...  9.34 us
    pallas_call x1, Pallas kernels, local(): pl.pallas_call(functools.partial(field_kernel, (depth, tiles, parts, stri...  6.41 us
    ppermute x5, starting transfers between devices, partner(): lax.ppermute(values, axis, [(n, n ^ bits) for n in range(lax.axis_size(ax...  6.08 us
    pallas_call x1, Pallas kernels, local(): pl.pallas_call(functools.partial(splat_kernel, tiles, parts), out_shape=j...  2.64 us
  transfers between devices with their start and end apart: 5, of which 4 were waited for; matrix products, arithmetic and copies ran while one was open for 0% of the time, Pallas kernels for 1%

profile of v1, /device:TPU:0, one launch (start us, length us, event | category | flops | bytes accessed | tf_op | source)
XLA Modules:
  0.0 36.1 jit_solution(5589658040397981370)
XLA Ops:
  0.6 2.6 %splat.1 = s16[160,640]{1,0:T(8,128)(2,1)} custom-call(s32[32,128]{1,0:T(8,128)} %bitcast.4, s32[32,128]{1,0:T(8,128)} %bitcast.6, f32[2,4096]{1,0:T(2,128)} %fracs_ref.1, f32[32,128]{1,0:T(8,128)} %bitcast.9, f32[640,128]{1,0:T(8,128)} %bitcast.8, s32[4,640]{1,0:T(4,128)} %cap_in.1, f32[4,640]{1,0:T(4,128)} %block_in.1), custom_call_target="tpu_custom_call" | custom-call | tf_op jit(solution)/shard_map/splat/pallas_call | solution.py:415
  3.3 10.5 %all_gather.3.refs_0_.refs_1_.refs_2_.refs_3_.codes_ref = s16[640,640]{1,0:T(8,128)(2,1)S(1)} all-gather(s16[160,640]{1,0:T(8,128)(2,1)} %splat.1), channel_id=1, replica_groups=mesh['strip'=8,'cells'=4] {'cells'}, dimensions={0}, use_global_device_ids=true | all-gather | bytes 1024000 | tf_op jit(solution)/shard_map/all_gather | solution.py:424
  13.7 0.1 sum_terms.1.refs_0_
  13.9 0.0 copy-start
  13.9 0.0 copy-start.1
  13.9 0.0 copy-start.2
  13.9 0.0 copy-start.3
  13.9 1.6 %collective-permute-start = (s16[16,640]{1,0:T(8,128)(2,1)S(1)}, s16[16,640]{1,0:T(8,128)(2,1)S(1)}, u32[]{:S(2)}, u32[]{:S(2)}) collective-permute-start(s16[16,640]{1,0:T(8,128)(2,1)S(1)} %sum_terms.1.refs_0_), channel_id=1, source_target_pairs={{0,8},{4,12},{8,0},{12,4},{16,24},{20,28},{24,16},{28,20},{1,9},{5... | collective-permute-start | bytes 61448 | tf_op jit(solution)/shard_map/ppermute | solution.py:395
  15.5 2.6 %collective-permute-start.1 = (s16[16,640]{1,0:T(8,128)(2,1)S(1)}, s16[16,640]{1,0:T(8,128)(2,1)S(1)}, u32[]{:S(2)}, u32[]{:S(2)}) collective-permute-start(s16[16,640]{1,0:T(8,128)(2,1)S(1)} %sum_terms.1.refs_0_), channel_id=1, source_target_pairs={{0,16},{4,20},{8,24},{12,28},{16,0},{20,4},{24,8},{28,12},{1,17},{... | collective-permute-start | bytes 61448 | tf_op jit(solution)/shard_map/ppermute | solution.py:395
  18.1 0.2 collective-permute-start.2
  18.4 0.0 collective-permute-done.refs_1_
  18.4 2.0 %collective-permute-done.1.refs_2_ = s16[16,640]{1,0:T(8,128)(2,1)S(1)} collective-permute-done((s16[16,640]{1,0:T(8,128)(2,1)S(1)}, s16[16,640]{1,0:T(8,128)(2,1)S(1)}, u32[]{:S(2)}, u32[]{:S(2)}) %collective-permute-start.1) | collective-permute-done | bytes 20512 | tf_op jit(solution)/shard_map/ppermute | solution.py:395
  20.3 3.4 %collective-permute-done.2.refs_3_ = s16[16,640]{1,0:T(8,128)(2,1)S(1)} collective-permute-done((s16[16,640]{1,0:T(8,128)(2,1)S(1)}, s16[16,640]{1,0:T(8,128)(2,1)S(1)}, u32[]{:S(2)}, u32[]{:S(2)}) %collective-permute-start.2) | collective-permute-done | bytes 20512 | tf_op jit(solution)/shard_map/ppermute | solution.py:395
  23.7 1.6 %collective-permute-start.3 = (s16[64,640]{1,0:T(8,128)(2,1)S(1)}, s16[64,640]{1,0:T(8,128)(2,1)S(1)}, u32[]{:S(2)}, u32[]{:S(2)}) collective-permute-start(s16[64,640]{1,0:T(8,128)(2,1)S(1)} %join.2.refs_0_), channel_id=1, source_target_pairs={{0,4},{4,0},{8,12},{12,8},{16,20},{20,16},{24,28},{28,24},{1,5},{5... | collective-permute-start | bytes 245768 | tf_op jit(solution)/shard_map/ppermute | solution.py:395
  25.3 2.9 %collective-permute-done.3.refs_1_ = s16[64,640]{1,0:T(8,128)(2,1)S(1)} collective-permute-done((s16[64,640]{1,0:T(8,128)(2,1)S(1)}, s16[64,640]{1,0:T(8,128)(2,1)S(1)}, u32[]{:S(2)}, u32[]{:S(2)}) %collective-permute-start.3) | collective-permute-done | bytes 81952 | tf_op jit(solution)/shard_map/ppermute | solution.py:395
  28.3 0.1 collective-permute-start.4
  28.3 0.3 unpack.1.pairs
  28.7 1.0 %collective-permute-done.4.refs_1_ = s16[128,640]{1,0:T(8,128)(2,1)S(1)} collective-permute-done((s16[128,640]{1,0:T(8,128)(2,1)S(1)}, s16[128,640]{1,0:T(8,128)(2,1)S(1)}, u32[]{:S(2)}, u32[]{:S(2)}) %collective-permute-start.4) | collective-permute-done | bytes 163872 | tf_op jit(solution)/shard_map/ppermute | solution.py:395
  29.7 0.0 copy-done
  29.7 0.0 copy-done.1
  29.7 0.0 copy-done.2
  29.7 0.0 copy-done.3
  29.7 6.4 %field.1 = (f32[4,640]{1,0:T(4,128)}, f32[2,4096]{1,0:T(2,128)}) custom-call(bf16[20,256,128]{2,1,0:T(8,128)(2,1)S(1)} %unpack.1.pairs, f32[1,32,32]{2,1,0:T(8,128)S(1)} %copy-done.3, s32[32,128]{1,0:T(8,128)S(1)} %bitcast.5, s32[32,128]{1,0:T(8,128)S(1)} %bitcast.7, f32[2,4096]{1,0:T(2,128)S(1)} %copy-done, s16[128,640]{1,0:T(8,128)(2,1)S(1)} %join.3.refs_0_, ...), custom_call_target="tpu_custom_call" | custom-call | tf_op jit(solution)/shard_map/field/pallas_call | solution.py:470
  (2 shorter events, 0.0 us)
Async XLA Ops:
  13.9 15.9 %copy-start = (f32[2,4096]{1,0:T(2,128)S(1)}, f32[2,4096]{1,0:T(2,128)}, u32[]{:S(2)}) copy-start(f32[2,4096]{1,0:T(2,128)} %fracs_ref.1) | copy-start | bytes 98308
  13.9 15.8 %copy-start.1 = (s32[4096]{0:T(1024)S(1)}, s32[4096]{0:T(1024)}, u32[]{:S(2)}) copy-start(s32[4096]{0:T(1024)} %param.8) | copy-start | bytes 49156
  13.9 15.8 %copy-start.2 = (s32[4096]{0:T(1024)S(1)}, s32[4096]{0:T(1024)}, u32[]{:S(2)}) copy-start(s32[4096]{0:T(1024)} %param.9) | copy-start | bytes 49156
  13.9 15.8 %copy-start.3 = (f32[1,32,32]{2,1,0:T(8,128)S(1)}, f32[1,32,32]{2,1,0:T(8,128)}, u32[]{:S(2)}) copy-start(f32[1,32,32]{2,1,0:T(8,128)} %col_blocks_ref.1) | copy-start | bytes 12292
  13.9 4.5 %collective-permute-start = (s16[16,640]{1,0:T(8,128)(2,1)S(1)}, s16[16,640]{1,0:T(8,128)(2,1)S(1)}, u32[]{:S(2)}, u32[]{:S(2)}) collective-permute-start(s16[16,640]{1,0:T(8,128)(2,1)S(1)} %sum_terms.1.refs_0_), channel_id=1, source_target_pairs={{0,8},{4,12},{8,0},{12,4},{16,24},{20,28},{24,16},{28,20},{1,9},{5... | collective-permute-start | bytes 61448 | tf_op jit(solution)/shard_map/ppermute | solution.py:395
  15.5 4.8 %collective-permute-start.1 = (s16[16,640]{1,0:T(8,128)(2,1)S(1)}, s16[16,640]{1,0:T(8,128)(2,1)S(1)}, u32[]{:S(2)}, u32[]{:S(2)}) collective-permute-start(s16[16,640]{1,0:T(8,128)(2,1)S(1)} %sum_terms.1.refs_0_), channel_id=1, source_target_pairs={{0,16},{4,20},{8,24},{12,28},{16,0},{20,4},{24,8},{28,12},{1,17},{... | collective-permute-start | bytes 61448 | tf_op jit(solution)/shard_map/ppermute | solution.py:395
  18.1 5.6 %collective-permute-start.2 = (s16[16,640]{1,0:T(8,128)(2,1)S(1)}, s16[16,640]{1,0:T(8,128)(2,1)S(1)}, u32[]{:S(2)}, u32[]{:S(2)}) collective-permute-start(s16[16,640]{1,0:T(8,128)(2,1)S(1)} %sum_terms.1.refs_0_), channel_id=1, source_target_pairs={{0,24},{4,28},{8,16},{12,20},{16,8},{20,12},{24,0},{28,4},{1,25},{... | collective-permute-start | bytes 61448 | tf_op jit(solution)/shard_map/ppermute | solution.py:395
  23.7 4.5 %collective-permute-start.3 = (s16[64,640]{1,0:T(8,128)(2,1)S(1)}, s16[64,640]{1,0:T(8,128)(2,1)S(1)}, u32[]{:S(2)}, u32[]{:S(2)}) collective-permute-start(s16[64,640]{1,0:T(8,128)(2,1)S(1)} %join.2.refs_0_), channel_id=1, source_target_pairs={{0,4},{4,0},{8,12},{12,8},{16,20},{20,16},{24,28},{28,24},{1,5},{5... | collective-permute-start | bytes 245768 | tf_op jit(solution)/shard_map/ppermute | solution.py:395
  28.3 1.5 %collective-permute-start.4 = (s16[128,640]{1,0:T(8,128)(2,1)S(1)}, s16[128,640]{1,0:T(8,128)(2,1)S(1)}, u32[]{:S(2)}, u32[]{:S(2)}) collective-permute-start(s16[128,640]{1,0:T(8,128)(2,1)S(1)} %join.3.refs_0_), channel_id=1, source_target_pairs={{0,1},{1,0},{2,3},{3,2},{4,5},{5,4},{6,7},{7,6},{8,9},{9,8},{10,11... | collective-permute-start | bytes 491528 | tf_op jit(solution)/shard_map/ppermute | solution.py:395

commit v2 on v0

--- a/solution.py
+++ b/solution.py
@@ -206,13 +206,13 @@
     for k in range(pairs_ref.shape[0]):
         base = (k // tiles) * (carried + LANES) + carried
         code = codes_ref[base : base + LANES, k % tiles * LANES : (k % tiles + 1) * LANES].astype(f32)
-        high, low = halves((code + code_half) * (block_span / code_top) + block_low)
-        pairs_ref[k, :LANES, :] = high
-        pairs_ref[k, LANES:, :] = low
+        high, low = halves(((code + code_half) * (block_span / code_top) + block_low).T)
+        pairs_ref[k, :, :LANES] = high
+        pairs_ref[k, :, LANES:] = low
 
 
 def field_kernel(
-    sizes, pairs, col_blocks_ref, rows_ref, cols_ref, fracs_ref, *refs,
+    sizes, orders, pairs, col_blocks_ref, rows_ref, cols_ref, fracs_ref, *refs,
 ):
     depth, tiles, parts, strips = sizes
     sent_refs, (final_ref, velocity_ref, weights_ref, source_ref, field_ref, ordered) = refs[:-6], refs[-6:]
@@ -228,9 +228,9 @@
         sent = sent_refs[0]
     else:
         sent = ordered
-        for near, sent_ref in enumerate(sent_refs):
-            for n in range(strips // 2):
-                ordered[strip ^ (2 * n + near)] = sent_ref[n * 2 * slots : (n + 1) * 2 * slots, :]
+        for order, sent_ref in zip(orders, sent_refs):
+            for n, bits in enumerate(order):
+                ordered[strip ^ bits] = sent_ref[n * 2 * slots : (n + 1) * 2 * slots, :]
     group = chunk // depth
     target, origin = iota((parts * chunk, group * slots), 0), iota((parts * chunk, group * slots), 1)
     slot = origin % slots
@@ -290,7 +290,8 @@
                 def multiply(t):
                     cut = row_tiles[t]
                     now = weights_ref[here, cut] * turned.tiles[t] + coupling * turned.along(t)
-                    return last_dims(jnp.concatenate(halves(source_ref[here, cut] - now), 0), pairs[t])
+                    both = jnp.concatenate(halves(source_ref[here, cut] - now), 0)
+                    return jnp.dot(both, pairs[t], preferred_element_type=f32)
 
                 def add(t, product):
                     high, low = product[:chunk], product[chunk:]
@@ -426,22 +427,24 @@
         name="sum_terms",
     )(*[blocks] * parts)
     if strips == 8:
-        from_z = {k: partner(sums, "strip", k) for k in (6, 4, 2)}
+        orders = ((0,), (1,), (6, 4, 2), (7, 5, 3))
+        from_z = [partner(sums, "strip", bits) for bits in (6, 4, 2)]
+        *from_z, near = lax.optimization_barrier((*from_z, partner(sums, "strip", 1)))
         held = pl.pallas_call(
             join_kernel,
-            out_shape=jax.ShapeDtypeStruct((strips // 2 * carried, width_part), jnp.int16),
-            in_specs=[vmem] * 4,
+            out_shape=jax.ShapeDtypeStruct((3 * carried, width_part), jnp.int16),
+            in_specs=[vmem] * 3,
             out_specs=vmem,
             compiler_params=small,
             name="join",
-        )(sums, from_z[2], from_z[4], from_z[6])
+        )(*from_z)
         held, blocks = lax.optimization_barrier((held, blocks))
-        sent = [held, partner(held, "strip", 1)]
+        sent = [sums, near, held, partner(held, "strip", 1)]
     else:
-        sent = [lax.all_gather(sums, "strip", axis=0)]
+        orders, sent = (), [lax.all_gather(sums, "strip", axis=0)]
     pairs = pl.pallas_call(
         functools.partial(unpack_kernel, tiles, carried),
-        out_shape=jax.ShapeDtypeStruct((width // LANES, 2 * LANES, LANES), bf16),
+        out_shape=jax.ShapeDtypeStruct((width // LANES, LANES, 2 * LANES), bf16),
         in_specs=[vmem],
         out_specs=vmem,
         compiler_params=small,
@@ -450,7 +453,7 @@
     )(blocks)
 
     final, velocity = pl.pallas_call(
-        functools.partial(field_kernel, (depth, tiles, parts, strips)),
+        functools.partial(field_kernel, (depth, tiles, parts, strips), orders),
         out_shape=(
             jax.ShapeDtypeStruct((depth, width_part), f32),
             jax.ShapeDtypeStruct((2, pins), f32),

time: 36 us -> 33.2 us (0.922)
  waiting for transfers between devices: 9.06 us -> 5.57 us
  starting transfers between devices: 6.01 us -> 7.5 us
  Pallas kernels: 9.51 us -> 8.71 us
    ppermute x4 -> x5, waiting for transfers between devices: 9.06 us -> 5.57 us  [partner(): lax.ppermute(values, axis, [(n, n ^ bits) for n in range(lax.axis_size(ax...]
    ppermute x4 -> x5, starting transfers between devices: 6.01 us -> 7.5 us  [partner(): lax.ppermute(values, axis, [(n, n ^ bits) for n in range(lax.axis_size(ax...]
    pallas_call x1, Pallas kernels: 6.43 us -> 5.51 us  [local(): pl.pallas_call(functools.partial(field_kernel, (depth, tiles, parts, stri...]
  transfers between devices with their start and end apart: 4 -> 5, of which waited for: 3 -> 2; matrix products, arithmetic and copies ran while one was open for 0% -> 0% of each run, Pallas kernels for 1% -> 1%
where the time goes in v2:
time: 33.2 us; the launch traced here: 33 us
  blocking collectives  10.5 us (32%)
  Pallas kernels  8.71 us (26%)
  starting transfers between devices  7.5 us (23%)
  waiting for transfers between devices  5.57 us (17%)
  between operations  0.7 us (2%)
    all_gather x1, blocking collectives, local(): blocks = lax.all_gather(terms, 'cells', axis=0, tiled=True)  10.5 us
    ppermute x5, starting transfers between devices, partner(): lax.ppermute(values, axis, [(n, n ^ bits) for n in range(lax.axis_size(ax...  7.5 us
    ppermute x5, waiting for transfers between devices, partner(): lax.ppermute(values, axis, [(n, n ^ bits) for n in range(lax.axis_size(ax...  5.57 us
    pallas_call x1, Pallas kernels, local(): pl.pallas_call(functools.partial(field_kernel, (depth, tiles, parts, stri...  5.51 us
    pallas_call x1, Pallas kernels, local(): pl.pallas_call(functools.partial(splat_kernel, tiles, parts), out_shape=j...  2.64 us
  transfers between devices with their start and end apart: 5, of which 2 were waited for; matrix products, arithmetic and copies ran while one was open for 0% of the time, Pallas kernels for 1%

profile of v2, /device:TPU:0, one launch (start us, length us, event | category | flops | bytes accessed | tf_op | source)
XLA Modules:
  0.0 33.0 jit_solution(7106396321662625379)
XLA Ops:
  0.6 2.6 %splat.1 = s16[160,640]{1,0:T(8,128)(2,1)} custom-call(s32[32,128]{1,0:T(8,128)} %bitcast.4, s32[32,128]{1,0:T(8,128)} %bitcast.6, f32[2,4096]{1,0:T(2,128)} %fracs_ref.1, f32[32,128]{1,0:T(8,128)} %bitcast.9, f32[640,128]{1,0:T(8,128)} %bitcast.8, s32[4,640]{1,0:T(4,128)} %cap_in.1, f32[4,640]{1,0:T(4,128)} %block_in.1), custom_call_target="tpu_custom_call" | custom-call | tf_op jit(solution)/shard_map/splat/pallas_call | solution.py:405
  3.3 10.5 %all_gather.3.refs_0_.refs_1_.refs_2_.refs_3_.codes_ref = s16[640,640]{1,0:T(8,128)(2,1)S(1)} all-gather(s16[160,640]{1,0:T(8,128)(2,1)} %splat.1), channel_id=1, replica_groups=mesh['strip'=8,'cells'=4] {'cells'}, dimensions={0}, use_global_device_ids=true | all-gather | bytes 1024000 | tf_op jit(solution)/shard_map/all_gather | solution.py:414
  13.7 0.1 sum_terms.1.refs_0_
  13.8 0.0 copy-start
  13.9 0.0 copy-start.1
  13.9 0.0 copy-start.2
  13.9 0.0 copy-start.3
  13.9 3.7 %collective-permute-start = (s16[32,640]{1,0:T(8,128)(2,1)S(1)}, s16[32,640]{1,0:T(8,128)(2,1)S(1)}, u32[]{:S(2)}, u32[]{:S(2)}) collective-permute-start(s16[32,640]{1,0:T(8,128)(2,1)S(1)} %sum_terms.1.refs_0_), channel_id=1, source_target_pairs={{0,24},{4,28},{8,16},{12,20},{16,8},{20,12},{24,0},{28,4},{1,25},{... | collective-permute-start | bytes 122888 | tf_op jit(solution)/shard_map/ppermute | solution.py:385
  17.6 0.0 collective-permute-start.1
  17.6 0.8 %collective-permute-start.2 = (s16[32,640]{1,0:T(8,128)(2,1)S(1)}, s16[32,640]{1,0:T(8,128)(2,1)S(1)}, u32[]{:S(2)}, u32[]{:S(2)}) collective-permute-start(s16[32,640]{1,0:T(8,128)(2,1)S(1)} %sum_terms.1.refs_0_), channel_id=1, source_target_pairs={{0,8},{4,12},{8,0},{12,4},{16,24},{20,28},{24,16},{28,20},{1,9},{5... | collective-permute-start | bytes 122888 | tf_op jit(solution)/shard_map/ppermute | solution.py:385
  18.4 1.5 %collective-permute-start.3 = (s16[32,640]{1,0:T(8,128)(2,1)S(1)}, s16[32,640]{1,0:T(8,128)(2,1)S(1)}, u32[]{:S(2)}, u32[]{:S(2)}) collective-permute-start(s16[32,640]{1,0:T(8,128)(2,1)S(1)} %sum_terms.1.refs_0_), channel_id=1, source_target_pairs={{0,4},{4,0},{8,12},{12,8},{16,20},{20,16},{24,28},{28,24},{1,5},{5... | collective-permute-start | bytes 122888 | tf_op jit(solution)/shard_map/ppermute | solution.py:385
  19.8 0.0 collective-permute-done.refs_0_
  19.8 2.6 %collective-permute-done.1.refs_1_ = s16[32,640]{1,0:T(8,128)(2,1)S(1)} collective-permute-done((s16[32,640]{1,0:T(8,128)(2,1)S(1)}, s16[32,640]{1,0:T(8,128)(2,1)S(1)}, u32[]{:S(2)}, u32[]{:S(2)}) %collective-permute-start.1) | collective-permute-done | bytes 40992 | tf_op jit(solution)/shard_map/ppermute | solution.py:385
  22.5 0.0 collective-permute-done.2.refs_2_
  22.5 0.0 collective-permute-done.3.refs_1_
  22.5 1.6 %collective-permute-start.4 = (s16[96,640]{1,0:T(8,128)(2,1)S(1)}, s16[96,640]{1,0:T(8,128)(2,1)S(1)}, u32[]{:S(2)}, u32[]{:S(2)}) collective-permute-start(s16[96,640]{1,0:T(8,128)(2,1)S(1)} %join.1.refs_2_), channel_id=1, source_target_pairs={{0,4},{4,0},{8,12},{12,8},{16,20},{20,16},{24,28},{28,24},{1,5},{5... | collective-permute-start | bytes 368648 | tf_op jit(solution)/shard_map/ppermute | solution.py:385
  24.0 0.4 %unpack.1.pairs = bf16[20,128,256]{2,1,0:T(8,128)(2,1)S(1)} custom-call(s16[640,640]{1,0:T(8,128)(2,1)S(1)} %all_gather.3.refs_0_.refs_1_.refs_2_.refs_3_.codes_ref), custom_call_target="tpu_custom_call" | custom-call | flops 1048576 | bytes 2097152 | tf_op jit(solution)/shard_map/unpack/pallas_call | solution.py:445
  24.5 2.9 %collective-permute-done.4.refs_3_ = s16[96,640]{1,0:T(8,128)(2,1)S(1)} collective-permute-done((s16[96,640]{1,0:T(8,128)(2,1)S(1)}, s16[96,640]{1,0:T(8,128)(2,1)S(1)}, u32[]{:S(2)}, u32[]{:S(2)}) %collective-permute-start.4) | collective-permute-done | bytes 122912 | tf_op jit(solution)/shard_map/ppermute | solution.py:385
  27.4 0.0 copy-done
  27.4 0.0 copy-done.1
  27.4 0.0 copy-done.2
  27.4 0.0 copy-done.3
  27.5 5.5 %field.1 = (f32[4,640]{1,0:T(4,128)}, f32[2,4096]{1,0:T(2,128)}) custom-call(bf16[20,128,256]{2,1,0:T(8,128)(2,1)S(1)} %unpack.1.pairs, f32[1,32,32]{2,1,0:T(8,128)S(1)} %copy-done.3, s32[32,128]{1,0:T(8,128)S(1)} %bitcast.5, s32[32,128]{1,0:T(8,128)S(1)} %bitcast.7, f32[2,4096]{1,0:T(2,128)S(1)} %copy-done, s16[32,640]{1,0:T(8,128)(2,1)S(1)} %sum_terms.1.refs_0_, ...), custom_call_target="tpu_custom_call" | custom-call | tf_op jit(solution)/shard_map/field/pallas_call | solution.py:455
  (1 shorter events, 0.0 us)
Async XLA Ops:
  13.8 13.6 %copy-start = (f32[2,4096]{1,0:T(2,128)S(1)}, f32[2,4096]{1,0:T(2,128)}, u32[]{:S(2)}) copy-start(f32[2,4096]{1,0:T(2,128)} %fracs_ref.1) | copy-start | bytes 98308
  13.9 13.6 %copy-start.1 = (s32[4096]{0:T(1024)S(1)}, s32[4096]{0:T(1024)}, u32[]{:S(2)}) copy-start(s32[4096]{0:T(1024)} %param.8) | copy-start | bytes 49156
  13.9 13.6 %copy-start.2 = (s32[4096]{0:T(1024)S(1)}, s32[4096]{0:T(1024)}, u32[]{:S(2)}) copy-start(s32[4096]{0:T(1024)} %param.9) | copy-start | bytes 49156
  13.9 13.6 %copy-start.3 = (f32[1,32,32]{2,1,0:T(8,128)S(1)}, f32[1,32,32]{2,1,0:T(8,128)}, u32[]{:S(2)}) copy-start(f32[1,32,32]{2,1,0:T(8,128)} %col_blocks_ref.1) | copy-start | bytes 12292
  13.9 5.9 %collective-permute-start = (s16[32,640]{1,0:T(8,128)(2,1)S(1)}, s16[32,640]{1,0:T(8,128)(2,1)S(1)}, u32[]{:S(2)}, u32[]{:S(2)}) collective-permute-start(s16[32,640]{1,0:T(8,128)(2,1)S(1)} %sum_terms.1.refs_0_), channel_id=1, source_target_pairs={{0,24},{4,28},{8,16},{12,20},{16,8},{20,12},{24,0},{28,4},{1,25},{... | collective-permute-start | bytes 122888 | tf_op jit(solution)/shard_map/ppermute | solution.py:385
  17.6 4.9 %collective-permute-start.1 = (s16[32,640]{1,0:T(8,128)(2,1)S(1)}, s16[32,640]{1,0:T(8,128)(2,1)S(1)}, u32[]{:S(2)}, u32[]{:S(2)}) collective-permute-start(s16[32,640]{1,0:T(8,128)(2,1)S(1)} %sum_terms.1.refs_0_), channel_id=1, source_target_pairs={{0,16},{4,20},{8,24},{12,28},{16,0},{20,4},{24,8},{28,12},{1,17},{... | collective-permute-start | bytes 122888 | tf_op jit(solution)/shard_map/ppermute | solution.py:385
  17.6 4.9 %collective-permute-start.2 = (s16[32,640]{1,0:T(8,128)(2,1)S(1)}, s16[32,640]{1,0:T(8,128)(2,1)S(1)}, u32[]{:S(2)}, u32[]{:S(2)}) collective-permute-start(s16[32,640]{1,0:T(8,128)(2,1)S(1)} %sum_terms.1.refs_0_), channel_id=1, source_target_pairs={{0,8},{4,12},{8,0},{12,4},{16,24},{20,28},{24,16},{28,20},{1,9},{5... | collective-permute-start | bytes 122888 | tf_op jit(solution)/shard_map/ppermute | solution.py:385
  18.4 4.1 %collective-permute-start.3 = (s16[32,640]{1,0:T(8,128)(2,1)S(1)}, s16[32,640]{1,0:T(8,128)(2,1)S(1)}, u32[]{:S(2)}, u32[]{:S(2)}) collective-permute-start(s16[32,640]{1,0:T(8,128)(2,1)S(1)} %sum_terms.1.refs_0_), channel_id=1, source_target_pairs={{0,4},{4,0},{8,12},{12,8},{16,20},{20,16},{24,28},{28,24},{1,5},{5... | collective-permute-start | bytes 122888 | tf_op jit(solution)/shard_map/ppermute | solution.py:385
  22.5 4.9 %collective-permute-start.4 = (s16[96,640]{1,0:T(8,128)(2,1)S(1)}, s16[96,640]{1,0:T(8,128)(2,1)S(1)}, u32[]{:S(2)}, u32[]{:S(2)}) collective-permute-start(s16[96,640]{1,0:T(8,128)(2,1)S(1)} %join.1.refs_2_), channel_id=1, source_target_pairs={{0,4},{4,0},{8,12},{12,8},{16,20},{20,16},{24,28},{28,24},{1,5},{5... | collective-permute-start | bytes 368648 | tf_op jit(solution)/shard_map/ppermute | solution.py:385

commit v3 on v2

--- a/solution.py
+++ b/solution.py
@@ -202,17 +202,38 @@
         refs[-1][n * ref.shape[0] : (n + 1) * ref.shape[0], :] = ref[...]
 
 
-def unpack_kernel(tiles, carried, codes_ref, pairs_ref):
+def tables_kernel(sizes, codes_ref, rows_ref, cols_ref, fracs_ref, pairs_ref, look_ref, share_ref):
+    depth, tiles, parts, carried = sizes
     for k in range(pairs_ref.shape[0]):
         base = (k // tiles) * (carried + LANES) + carried
         code = codes_ref[base : base + LANES, k % tiles * LANES : (k % tiles + 1) * LANES].astype(f32)
         high, low = halves(((code + code_half) * (block_span / code_top) + block_low).T)
         pairs_ref[k, :, :LANES] = high
         pairs_ref[k, :, LANES:] = low
+    half = LANES // 2
+    many = parts * tiles * depth
+    rows, cols = rows_ref[...], cols_ref[...]
+    blank = jnp.zeros((LANES - many, LANES), bf16)
+    keys, lane = iota((many, LANES), 0), iota((half + 8, LANES), 0)
+    for j in range(rows.shape[0]):
+        cut = slice(j * LANES, (j + 1) * LANES)
+        fy, fx = fracs_ref[0:1, cut], fracs_ref[1:2, cut]
+        col = cols[j : j + 1]
+        key = (col >> 7) * depth + rows[j : j + 1]
+        second = (col & half) != 0
+        near, far = rounded(1.0 - fy), rounded(fy)
+        looks = [
+            pick(keys, jnp.where(second, -8, key), near, far).astype(bf16),
+            blank,
+            pick(keys, jnp.where(second, key, -8), near, far).astype(bf16),
+            blank,
+        ]
+        look_ref[:, cut] = jnp.concatenate(looks, 0)
+        share_ref[:, cut] = pick(lane, col & (half - 1), rounded(1.0 - fx), rounded(fx))
 
 
 def field_kernel(
-    sizes, orders, pairs, col_blocks_ref, rows_ref, cols_ref, fracs_ref, *refs,
+    sizes, orders, pairs, look_ref, share_ref, col_blocks_ref, *refs,
 ):
     depth, tiles, parts, strips = sizes
     sent_refs, (final_ref, velocity_ref, weights_ref, source_ref, field_ref, ordered) = refs[:-6], refs[-6:]
@@ -356,27 +377,12 @@
         return jnp.concatenate([turned[: half + 8], jnp.concatenate([turned[half:], after], 0)], 1)
 
     table = jnp.concatenate([table_of(velocity_y), table_of(velocity_x)], 0).astype(bf16)
-    many = parts * tiles * depth
-    rows, cols = rows_ref[...], cols_ref[...]
-    joined = 2 if rows.shape[0] % 2 == 0 else 1
-    blank = jnp.zeros((LANES - many, joined * LANES), bf16)
-    keys, lane = iota((many, joined * LANES), 0), iota((half + 8, joined * LANES), 0)
-    for j in range(0, rows.shape[0], joined):
-        cut = slice(j * LANES, (j + joined) * LANES)
-        fy, fx = fracs_ref[0:1, cut], fracs_ref[1:2, cut]
-        col = jnp.concatenate([cols[n : n + 1] for n in range(j, j + joined)], 1)
-        row = jnp.concatenate([rows[n : n + 1] for n in range(j, j + joined)], 1)
-        key = (col >> 7) * depth + row
-        second = (col & half) != 0
-        near, far = rounded(1.0 - fy), rounded(fy)
-        looks = [
-            pick(keys, jnp.where(second, -8, key), near, far).astype(bf16),
-            blank,
-            pick(keys, jnp.where(second, key, -8), near, far).astype(bf16),
-            blank,
-        ]
-        sampled = jnp.dot(table, jnp.concatenate(looks, 0), preferred_element_type=f32)
-        share = pick(lane, col & (half - 1), rounded(1.0 - fx), rounded(fx))
+    pins = share_ref.shape[1]
+    at_once = 2 * LANES if pins % (2 * LANES) == 0 else LANES
+    for j in range(0, pins, at_once):
+        cut = slice(j, j + at_once)
+        sampled = jnp.dot(table, look_ref[:, cut], preferred_element_type=f32)
+        share = share_ref[:, cut]
         velocity_ref[0:1, cut] = jnp.sum(sampled[: half + 8] * share, 0, keepdims=True)
         velocity_ref[1:2, cut] = jnp.sum(sampled[half + 8 :] * share, 0, keepdims=True)
 
@@ -442,15 +448,19 @@
         sent = [sums, near, held, partner(held, "strip", 1)]
     else:
         orders, sent = (), [lax.all_gather(sums, "strip", axis=0)]
-    pairs = pl.pallas_call(
-        functools.partial(unpack_kernel, tiles, carried),
-        out_shape=jax.ShapeDtypeStruct((width // LANES, LANES, 2 * LANES), bf16),
-        in_specs=[vmem],
-        out_specs=vmem,
+    pairs, look, share = pl.pallas_call(
+        functools.partial(tables_kernel, (depth, tiles, parts, carried)),
+        out_shape=(
+            jax.ShapeDtypeStruct((width // LANES, LANES, 2 * LANES), bf16),
+            jax.ShapeDtypeStruct((2 * LANES, pins), bf16),
+            jax.ShapeDtypeStruct((LANES // 2 + 8, pins), f32),
+        ),
+        in_specs=[vmem] * 4,
+        out_specs=(vmem,) * 3,
         compiler_params=small,
         cost_estimate=pl.CostEstimate(flops=1 << 20, bytes_accessed=1 << 21, transcendentals=0),
-        name="unpack",
-    )(blocks)
+        name="tables",
+    )(blocks, rows, cols, pin_fracs)
 
     final, velocity = pl.pallas_call(
         functools.partial(field_kernel, (depth, tiles, parts, strips), orders),
@@ -458,7 +468,7 @@
             jax.ShapeDtypeStruct((depth, width_part), f32),
             jax.ShapeDtypeStruct((2, pins), f32),
         ),
-        in_specs=[vmem] * (5 + len(sent)),
+        in_specs=[vmem] * (4 + len(sent)),
         out_specs=(vmem, vmem),
         scratch_shapes=[
             pltpu.VMEM((height, width), f32),
@@ -468,7 +478,7 @@
         ],
         compiler_params=large,
         name="field",
-    )(pairs, col_blocks, rows, cols, pin_fracs, *sent)
+    )(pairs, look, share, col_blocks, *sent)
     return final, velocity
 
 

time: 33.2 us -> 32.5 us (0.979)
  waiting for transfers between devices: 5.57 us -> 4.56 us
    ppermute x5, waiting for transfers between devices: 5.57 us -> 4.56 us  [partner(): lax.ppermute(values, axis, [(n, n ^ bits) for n in range(lax.axis_size(ax...]
    pallas_call x1, Pallas kernels: 0.44 us -> 1.44 us  [local(): pl.pallas_call(functools.partial(tables_kernel, (depth, tiles, parts, car...]
    pallas_call x1, Pallas kernels: 5.51 us -> 4.84 us  [local(): pl.pallas_call(functools.partial(field_kernel, (depth, tiles, parts, stri...]
  transfers between devices with their start and end apart: 5 -> 5, of which waited for: 2 -> 2; matrix products, arithmetic and copies ran while one was open for 0% -> 0% of each run, Pallas kernels for 1% -> 4%
where the time goes in v3:
time: 32.5 us; the launch traced here: 32.2 us
  blocking collectives  10.5 us (32%)
  Pallas kernels  9.02 us (28%)
  starting transfers between devices  7.5 us (23%)
  waiting for transfers between devices  4.56 us (14%)
  between operations  0.67 us (2%)
    all_gather x1, blocking collectives, local(): blocks = lax.all_gather(terms, 'cells', axis=0, tiled=True)  10.5 us
    ppermute x5, starting transfers between devices, partner(): lax.ppermute(values, axis, [(n, n ^ bits) for n in range(lax.axis_size(ax...  7.5 us
    pallas_call x1, Pallas kernels, local(): pl.pallas_call(functools.partial(field_kernel, (depth, tiles, parts, stri...  4.84 us
    ppermute x5, waiting for transfers between devices, partner(): lax.ppermute(values, axis, [(n, n ^ bits) for n in range(lax.axis_size(ax...  4.56 us
    pallas_call x1, Pallas kernels, local(): pl.pallas_call(functools.partial(splat_kernel, tiles, parts), out_shape=j...  2.63 us
    pallas_call x1, Pallas kernels, local(): pl.pallas_call(functools.partial(tables_kernel, (depth, tiles, parts, car...  1.44 us
  transfers between devices with their start and end apart: 5, of which 2 were waited for; matrix products, arithmetic and copies ran while one was open for 0% of the time, Pallas kernels for 4%

profile of v3, /device:TPU:0, one launch (start us, length us, event | category | flops | bytes accessed | tf_op | source)
XLA Modules:
  0.0 32.2 jit_solution(14961858829156123772)
XLA Ops:
  0.6 2.6 %splat.1 = s16[160,640]{1,0:T(8,128)(2,1)} custom-call(s32[32,128]{1,0:T(8,128)} %bitcast.4, s32[32,128]{1,0:T(8,128)} %bitcast.6, f32[2,4096]{1,0:T(2,128)} %fracs_ref.1, f32[32,128]{1,0:T(8,128)} %bitcast.9, f32[640,128]{1,0:T(8,128)} %bitcast.8, s32[4,640]{1,0:T(4,128)} %cap_in.1, f32[4,640]{1,0:T(4,128)} %block_in.1), custom_call_target="tpu_custom_call" | custom-call | tf_op jit(solution)/shard_map/splat/pallas_call | solution.py:411
  3.3 10.5 %all_gather.3.refs_0_.refs_1_.refs_2_.refs_3_.codes_ref = s16[640,640]{1,0:T(8,128)(2,1)S(1)} all-gather(s16[160,640]{1,0:T(8,128)(2,1)} %splat.1), channel_id=1, replica_groups=mesh['strip'=8,'cells'=4] {'cells'}, dimensions={0}, use_global_device_ids=true | all-gather | bytes 1024000 | tf_op jit(solution)/shard_map/all_gather | solution.py:420
  13.7 0.0 copy-start
  13.7 0.0 copy-start.1
  13.7 0.0 copy-start.2
  13.7 0.0 copy-start.3
  13.7 0.1 sum_terms.1.refs_0_
  13.9 3.7 %collective-permute-start = (s16[32,640]{1,0:T(8,128)(2,1)S(1)}, s16[32,640]{1,0:T(8,128)(2,1)S(1)}, u32[]{:S(2)}, u32[]{:S(2)}) collective-permute-start(s16[32,640]{1,0:T(8,128)(2,1)S(1)} %sum_terms.1.refs_0_), channel_id=1, source_target_pairs={{0,24},{4,28},{8,16},{12,20},{16,8},{20,12},{24,0},{28,4},{1,25},{... | collective-permute-start | bytes 122888 | tf_op jit(solution)/shard_map/ppermute | solution.py:391
  17.5 0.0 collective-permute-start.1
  17.5 0.8 %collective-permute-start.2 = (s16[32,640]{1,0:T(8,128)(2,1)S(1)}, s16[32,640]{1,0:T(8,128)(2,1)S(1)}, u32[]{:S(2)}, u32[]{:S(2)}) collective-permute-start(s16[32,640]{1,0:T(8,128)(2,1)S(1)} %sum_terms.1.refs_0_), channel_id=1, source_target_pairs={{0,8},{4,12},{8,0},{12,4},{16,24},{20,28},{24,16},{28,20},{1,9},{5... | collective-permute-start | bytes 122888 | tf_op jit(solution)/shard_map/ppermute | solution.py:391
  18.3 1.5 %collective-permute-start.3 = (s16[32,640]{1,0:T(8,128)(2,1)S(1)}, s16[32,640]{1,0:T(8,128)(2,1)S(1)}, u32[]{:S(2)}, u32[]{:S(2)}) collective-permute-start(s16[32,640]{1,0:T(8,128)(2,1)S(1)} %sum_terms.1.refs_0_), channel_id=1, source_target_pairs={{0,4},{4,0},{8,12},{12,8},{16,20},{20,16},{24,28},{28,24},{1,5},{5... | collective-permute-start | bytes 122888 | tf_op jit(solution)/shard_map/ppermute | solution.py:391
  19.8 0.0 collective-permute-done.refs_0_
  19.8 2.6 %collective-permute-done.1.refs_1_ = s16[32,640]{1,0:T(8,128)(2,1)S(1)} collective-permute-done((s16[32,640]{1,0:T(8,128)(2,1)S(1)}, s16[32,640]{1,0:T(8,128)(2,1)S(1)}, u32[]{:S(2)}, u32[]{:S(2)}) %collective-permute-start.1) | collective-permute-done | bytes 40992 | tf_op jit(solution)/shard_map/ppermute | solution.py:391
  22.4 0.0 collective-permute-done.2.refs_2_
  22.4 0.0 collective-permute-done.3.refs_1_
  22.4 1.6 %collective-permute-start.4 = (s16[96,640]{1,0:T(8,128)(2,1)S(1)}, s16[96,640]{1,0:T(8,128)(2,1)S(1)}, u32[]{:S(2)}, u32[]{:S(2)}) collective-permute-start(s16[96,640]{1,0:T(8,128)(2,1)S(1)} %join.1.refs_2_), channel_id=1, source_target_pairs={{0,4},{4,0},{8,12},{12,8},{16,20},{20,16},{24,28},{28,24},{1,5},{5... | collective-permute-start | bytes 368648 | tf_op jit(solution)/shard_map/ppermute | solution.py:391
  24.0 0.0 copy-done
  24.0 0.0 copy-done.1
  24.0 0.0 copy-done.2
  24.0 1.4 %tables.1 = (bf16[20,128,256]{2,1,0:T(8,128)(2,1)S(1)}, bf16[256,4096]{1,0:T(8,128)(2,1)S(1)}, f32[72,4096]{1,0:T(8,128)S(1)}) custom-call(s16[640,640]{1,0:T(8,128)(2,1)S(1)} %all_gather.3.refs_0_.refs_1_.refs_2_.refs_3_.codes_ref, s32[32,128]{1,0:T(8,128)S(1)} %bitcast.5, s32[32,128]{1,0:T(8,128)S(1)} %bitcast.7, f32[2,4096]{1,0:T(2,128)S(1)} %copy-done), custom_call_target="tpu_custom_call" | custom-call | flops 1048576 | bytes 2097152 | tf_op jit(solution)/shard_map/tables/pallas_call | solution.py:451
  25.5 1.9 %collective-permute-done.4.refs_3_ = s16[96,640]{1,0:T(8,128)(2,1)S(1)} collective-permute-done((s16[96,640]{1,0:T(8,128)(2,1)S(1)}, s16[96,640]{1,0:T(8,128)(2,1)S(1)}, u32[]{:S(2)}, u32[]{:S(2)}) %collective-permute-start.4) | collective-permute-done | bytes 122912 | tf_op jit(solution)/shard_map/ppermute | solution.py:391
  27.4 0.0 copy-done.3
  27.4 4.8 %field.1 = (f32[4,640]{1,0:T(4,128)}, f32[2,4096]{1,0:T(2,128)}) custom-call(bf16[20,128,256]{2,1,0:T(8,128)(2,1)S(1)} %get-tuple-element.15.pairs, bf16[256,4096]{1,0:T(8,128)(2,1)S(1)} %get-tuple-element.16.look_ref, f32[72,4096]{1,0:T(8,128)S(1)} %get-tuple-element.17.share_ref, f32[1,32,32]{2,1,0:T(8,128)S(1)} %copy-done.3, ...), custom_call_target="tpu_custom_call" | custom-call | tf_op jit(solution)/shard_map/field/pallas_call | solution.py:465
  (1 shorter events, 0.0 us)
Async XLA Ops:
  13.7 10.3 %copy-start = (f32[2,4096]{1,0:T(2,128)S(1)}, f32[2,4096]{1,0:T(2,128)}, u32[]{:S(2)}) copy-start(f32[2,4096]{1,0:T(2,128)} %fracs_ref.1) | copy-start | bytes 98308
  13.7 10.3 %copy-start.1 = (s32[4096]{0:T(1024)S(1)}, s32[4096]{0:T(1024)}, u32[]{:S(2)}) copy-start(s32[4096]{0:T(1024)} %param.8) | copy-start | bytes 49156
  13.7 10.3 %copy-start.2 = (s32[4096]{0:T(1024)S(1)}, s32[4096]{0:T(1024)}, u32[]{:S(2)}) copy-start(s32[4096]{0:T(1024)} %param.9) | copy-start | bytes 49156
  13.7 13.7 %copy-start.3 = (f32[1,32,32]{2,1,0:T(8,128)S(1)}, f32[1,32,32]{2,1,0:T(8,128)}, u32[]{:S(2)}) copy-start(f32[1,32,32]{2,1,0:T(8,128)} %col_blocks_ref.1) | copy-start | bytes 12292
  13.9 5.9 %collective-permute-start = (s16[32,640]{1,0:T(8,128)(2,1)S(1)}, s16[32,640]{1,0:T(8,128)(2,1)S(1)}, u32[]{:S(2)}, u32[]{:S(2)}) collective-permute-start(s16[32,640]{1,0:T(8,128)(2,1)S(1)} %sum_terms.1.refs_0_), channel_id=1, source_target_pairs={{0,24},{4,28},{8,16},{12,20},{16,8},{20,12},{24,0},{28,4},{1,25},{... | collective-permute-start | bytes 122888 | tf_op jit(solution)/shard_map/ppermute | solution.py:391
  17.5 4.9 %collective-permute-start.1 = (s16[32,640]{1,0:T(8,128)(2,1)S(1)}, s16[32,640]{1,0:T(8,128)(2,1)S(1)}, u32[]{:S(2)}, u32[]{:S(2)}) collective-permute-start(s16[32,640]{1,0:T(8,128)(2,1)S(1)} %sum_terms.1.refs_0_), channel_id=1, source_target_pairs={{0,16},{4,20},{8,24},{12,28},{16,0},{20,4},{24,8},{28,12},{1,17},{... | collective-permute-start | bytes 122888 | tf_op jit(solution)/shard_map/ppermute | solution.py:391
  17.5 4.9 %collective-permute-start.2 = (s16[32,640]{1,0:T(8,128)(2,1)S(1)}, s16[32,640]{1,0:T(8,128)(2,1)S(1)}, u32[]{:S(2)}, u32[]{:S(2)}) collective-permute-start(s16[32,640]{1,0:T(8,128)(2,1)S(1)} %sum_terms.1.refs_0_), channel_id=1, source_target_pairs={{0,8},{4,12},{8,0},{12,4},{16,24},{20,28},{24,16},{28,20},{1,9},{5... | collective-permute-start | bytes 122888 | tf_op jit(solution)/shard_map/ppermute | solution.py:391
  18.3 4.1 %collective-permute-start.3 = (s16[32,640]{1,0:T(8,128)(2,1)S(1)}, s16[32,640]{1,0:T(8,128)(2,1)S(1)}, u32[]{:S(2)}, u32[]{:S(2)}) collective-permute-start(s16[32,640]{1,0:T(8,128)(2,1)S(1)} %sum_terms.1.refs_0_), channel_id=1, source_target_pairs={{0,4},{4,0},{8,12},{12,8},{16,20},{20,16},{24,28},{28,24},{1,5},{5... | collective-permute-start | bytes 122888 | tf_op jit(solution)/shard_map/ppermute | solution.py:391
  22.4 4.9 %collective-permute-start.4 = (s16[96,640]{1,0:T(8,128)(2,1)S(1)}, s16[96,640]{1,0:T(8,128)(2,1)S(1)}, u32[]{:S(2)}, u32[]{:S(2)}) collective-permute-start(s16[96,640]{1,0:T(8,128)(2,1)S(1)} %join.1.refs_2_), channel_id=1, source_target_pairs={{0,4},{4,0},{8,12},{12,8},{16,20},{20,16},{24,28},{28,24},{1,5},{5... | collective-permute-start | bytes 368648 | tf_op jit(solution)/shard_map/ppermute | solution.py:391

commit v4 on v3

--- a/solution.py
+++ b/solution.py
@@ -433,19 +433,18 @@
         name="sum_terms",
     )(*[blocks] * parts)
     if strips == 8:
-        orders = ((0,), (1,), (6, 4, 2), (7, 5, 3))
-        from_z = [partner(sums, "strip", bits) for bits in (6, 4, 2)]
-        *from_z, near = lax.optimization_barrier((*from_z, partner(sums, "strip", 1)))
+        orders = ((0, 6, 4, 2), (1, 7, 5, 3))
+        from_z = lax.optimization_barrier([partner(sums, "strip", bits) for bits in (6, 4, 2)])
         held = pl.pallas_call(
             join_kernel,
-            out_shape=jax.ShapeDtypeStruct((3 * carried, width_part), jnp.int16),
-            in_specs=[vmem] * 3,
+            out_shape=jax.ShapeDtypeStruct((4 * carried, width_part), jnp.int16),
+            in_specs=[vmem] * 4,
             out_specs=vmem,
             compiler_params=small,
             name="join",
-        )(*from_z)
+        )(sums, *from_z)
         held, blocks = lax.optimization_barrier((held, blocks))
-        sent = [sums, near, held, partner(held, "strip", 1)]
+        sent = [held, partner(held, "strip", 1)]
     else:
         orders, sent = (), [lax.all_gather(sums, "strip", axis=0)]
     pairs, look, share = pl.pallas_call(

time: 32.5 us -> 33.1 us (1.018)
  waiting for transfers between devices: 4.56 us -> 6.63 us
  starting transfers between devices: 7.5 us -> 6.01 us
    ppermute x5 -> x4, waiting for transfers between devices: 4.56 us -> 6.63 us  [partner(): lax.ppermute(values, axis, [(n, n ^ bits) for n in range(lax.axis_size(ax...]
    ppermute x5 -> x4, starting transfers between devices: 7.5 us -> 6.01 us  [partner(): lax.ppermute(values, axis, [(n, n ^ bits) for n in range(lax.axis_size(ax...]
  transfers between devices with their start and end apart: 5 -> 4, of which waited for: 2 -> 3; matrix products, arithmetic and copies ran while one was open for 0% -> 0% of each run, Pallas kernels for 4% -> 4%
where the time goes in v4:
time: 33.1 us; the launch traced here: 32.8 us
  blocking collectives  10.5 us (32%)
  Pallas kernels  9.04 us (27%)
  waiting for transfers between devices  6.63 us (20%)
  starting transfers between devices  6.01 us (18%)
  between operations  0.67 us (2%)
    all_gather x1, blocking collectives, local(): blocks = lax.all_gather(terms, 'cells', axis=0, tiled=True)  10.5 us
    ppermute x4, waiting for transfers between devices, partner(): lax.ppermute(values, axis, [(n, n ^ bits) for n in range(lax.axis_size(ax...  6.63 us
    ppermute x4, starting transfers between devices, partner(): lax.ppermute(values, axis, [(n, n ^ bits) for n in range(lax.axis_size(ax...  6.01 us
    pallas_call x1, Pallas kernels, local(): pl.pallas_call(functools.partial(field_kernel, (depth, tiles, parts, stri...  4.84 us
    pallas_call x1, Pallas kernels, local(): pl.pallas_call(functools.partial(splat_kernel, tiles, parts), out_shape=j...  2.64 us
    pallas_call x1, Pallas kernels, local(): pl.pallas_call(functools.partial(tables_kernel, (depth, tiles, parts, car...  1.43 us
  transfers between devices with their start and end apart: 4, of which 3 were waited for; matrix products, arithmetic and copies ran while one was open for 0% of the time, Pallas kernels for 4%

profile of v4, /device:TPU:0, one launch (start us, length us, event | category | flops | bytes accessed | tf_op | source)
XLA Modules:
  0.0 32.8 jit_solution(13373147832365736413)
XLA Ops:
  0.6 2.6 %splat.1 = s16[160,640]{1,0:T(8,128)(2,1)} custom-call(s32[32,128]{1,0:T(8,128)} %bitcast.4, s32[32,128]{1,0:T(8,128)} %bitcast.6, f32[2,4096]{1,0:T(2,128)} %fracs_ref.1, f32[32,128]{1,0:T(8,128)} %bitcast.9, f32[640,128]{1,0:T(8,128)} %bitcast.8, s32[4,640]{1,0:T(4,128)} %cap_in.1, f32[4,640]{1,0:T(4,128)} %block_in.1), custom_call_target="tpu_custom_call" | custom-call | tf_op jit(solution)/shard_map/splat/pallas_call | solution.py:411
  3.3 10.5 %all_gather.3.refs_0_.refs_1_.refs_2_.refs_3_.codes_ref = s16[640,640]{1,0:T(8,128)(2,1)S(1)} all-gather(s16[160,640]{1,0:T(8,128)(2,1)} %splat.1), channel_id=1, replica_groups=mesh['strip'=8,'cells'=4] {'cells'}, dimensions={0}, use_global_device_ids=true | all-gather | bytes 1024000 | tf_op jit(solution)/shard_map/all_gather | solution.py:420
  13.7 0.0 copy-start
  13.7 0.0 copy-start.1
  13.8 0.0 copy-start.2
  13.8 0.0 copy-start.3
  13.8 0.1 sum_terms.1.refs_0_
  13.9 3.7 %collective-permute-start = (s16[32,640]{1,0:T(8,128)(2,1)S(1)}, s16[32,640]{1,0:T(8,128)(2,1)S(1)}, u32[]{:S(2)}, u32[]{:S(2)}) collective-permute-start(s16[32,640]{1,0:T(8,128)(2,1)S(1)} %sum_terms.1.refs_0_), channel_id=1, source_target_pairs={{0,24},{4,28},{8,16},{12,20},{16,8},{20,12},{24,0},{28,4},{1,25},{... | collective-permute-start | bytes 122888 | tf_op jit(solution)/shard_map/ppermute | solution.py:391
  17.5 0.0 collective-permute-start.1
  17.5 0.8 %collective-permute-start.2 = (s16[32,640]{1,0:T(8,128)(2,1)S(1)}, s16[32,640]{1,0:T(8,128)(2,1)S(1)}, u32[]{:S(2)}, u32[]{:S(2)}) collective-permute-start(s16[32,640]{1,0:T(8,128)(2,1)S(1)} %sum_terms.1.refs_0_), channel_id=1, source_target_pairs={{0,8},{4,12},{8,0},{12,4},{16,24},{20,28},{24,16},{28,20},{1,9},{5... | collective-permute-start | bytes 122888 | tf_op jit(solution)/shard_map/ppermute | solution.py:391
  18.3 1.5 %collective-permute-done.refs_1_ = s16[32,640]{1,0:T(8,128)(2,1)S(1)} collective-permute-done((s16[32,640]{1,0:T(8,128)(2,1)S(1)}, s16[32,640]{1,0:T(8,128)(2,1)S(1)}, u32[]{:S(2)}, u32[]{:S(2)}) %collective-permute-start) | collective-permute-done | bytes 40992 | tf_op jit(solution)/shard_map/ppermute | solution.py:391
  19.8 2.7 %collective-permute-done.1.refs_2_ = s16[32,640]{1,0:T(8,128)(2,1)S(1)} collective-permute-done((s16[32,640]{1,0:T(8,128)(2,1)S(1)}, s16[32,640]{1,0:T(8,128)(2,1)S(1)}, u32[]{:S(2)}, u32[]{:S(2)}) %collective-permute-start.1) | collective-permute-done | bytes 40992 | tf_op jit(solution)/shard_map/ppermute | solution.py:391
  22.4 0.0 collective-permute-done.2.refs_3_
  22.5 1.6 %collective-permute-start.3 = (s16[128,640]{1,0:T(8,128)(2,1)S(1)}, s16[128,640]{1,0:T(8,128)(2,1)S(1)}, u32[]{:S(2)}, u32[]{:S(2)}) collective-permute-start(s16[128,640]{1,0:T(8,128)(2,1)S(1)} %join.1.refs_0_), channel_id=1, source_target_pairs={{0,4},{4,0},{8,12},{12,8},{16,20},{20,16},{24,28},{28,24},{1,5},{5... | collective-permute-start | bytes 491528 | tf_op jit(solution)/shard_map/ppermute | solution.py:391
  24.0 0.0 copy-done
  24.0 0.0 copy-done.1
  24.0 0.0 copy-done.2
  24.0 1.4 %tables.1 = (bf16[20,128,256]{2,1,0:T(8,128)(2,1)S(1)}, bf16[256,4096]{1,0:T(8,128)(2,1)S(1)}, f32[72,4096]{1,0:T(8,128)S(1)}) custom-call(s16[640,640]{1,0:T(8,128)(2,1)S(1)} %all_gather.3.refs_0_.refs_1_.refs_2_.refs_3_.codes_ref, s32[32,128]{1,0:T(8,128)S(1)} %bitcast.5, s32[32,128]{1,0:T(8,128)S(1)} %bitcast.7, f32[2,4096]{1,0:T(2,128)S(1)} %copy-done), custom_call_target="tpu_custom_call" | custom-call | flops 1048576 | bytes 2097152 | tf_op jit(solution)/shard_map/tables/pallas_call | solution.py:450
  25.5 2.5 %collective-permute-done.3.refs_1_ = s16[128,640]{1,0:T(8,128)(2,1)S(1)} collective-permute-done((s16[128,640]{1,0:T(8,128)(2,1)S(1)}, s16[128,640]{1,0:T(8,128)(2,1)S(1)}, u32[]{:S(2)}, u32[]{:S(2)}) %collective-permute-start.3) | collective-permute-done | bytes 163872 | tf_op jit(solution)/shard_map/ppermute | solution.py:391
  28.0 0.0 copy-done.3
  28.0 4.8 %field.1 = (f32[4,640]{1,0:T(4,128)}, f32[2,4096]{1,0:T(2,128)}) custom-call(bf16[20,128,256]{2,1,0:T(8,128)(2,1)S(1)} %get-tuple-element.14.pairs, bf16[256,4096]{1,0:T(8,128)(2,1)S(1)} %get-tuple-element.15.look_ref, f32[72,4096]{1,0:T(8,128)S(1)} %get-tuple-element.16.share_ref, f32[1,32,32]{2,1,0:T(8,128)S(1)} %copy-done.3, ...), custom_call_target="tpu_custom_call" | custom-call | tf_op jit(solution)/shard_map/field/pallas_call | solution.py:464
  (1 shorter events, 0.0 us)
Async XLA Ops:
  13.7 10.3 %copy-start = (f32[2,4096]{1,0:T(2,128)S(1)}, f32[2,4096]{1,0:T(2,128)}, u32[]{:S(2)}) copy-start(f32[2,4096]{1,0:T(2,128)} %fracs_ref.1) | copy-start | bytes 98308
  13.7 10.3 %copy-start.1 = (s32[4096]{0:T(1024)S(1)}, s32[4096]{0:T(1024)}, u32[]{:S(2)}) copy-start(s32[4096]{0:T(1024)} %param.8) | copy-start | bytes 49156
  13.8 10.3 %copy-start.2 = (s32[4096]{0:T(1024)S(1)}, s32[4096]{0:T(1024)}, u32[]{:S(2)}) copy-start(s32[4096]{0:T(1024)} %param.9) | copy-start | bytes 49156
  13.8 14.2 %copy-start.3 = (f32[1,32,32]{2,1,0:T(8,128)S(1)}, f32[1,32,32]{2,1,0:T(8,128)}, u32[]{:S(2)}) copy-start(f32[1,32,32]{2,1,0:T(8,128)} %col_blocks_ref.1) | copy-start | bytes 12292
  13.9 5.9 %collective-permute-start = (s16[32,640]{1,0:T(8,128)(2,1)S(1)}, s16[32,640]{1,0:T(8,128)(2,1)S(1)}, u32[]{:S(2)}, u32[]{:S(2)}) collective-permute-start(s16[32,640]{1,0:T(8,128)(2,1)S(1)} %sum_terms.1.refs_0_), channel_id=1, source_target_pairs={{0,24},{4,28},{8,16},{12,20},{16,8},{20,12},{24,0},{28,4},{1,25},{... | collective-permute-start | bytes 122888 | tf_op jit(solution)/shard_map/ppermute | solution.py:391
  17.5 4.9 %collective-permute-start.1 = (s16[32,640]{1,0:T(8,128)(2,1)S(1)}, s16[32,640]{1,0:T(8,128)(2,1)S(1)}, u32[]{:S(2)}, u32[]{:S(2)}) collective-permute-start(s16[32,640]{1,0:T(8,128)(2,1)S(1)} %sum_terms.1.refs_0_), channel_id=1, source_target_pairs={{0,16},{4,20},{8,24},{12,28},{16,0},{20,4},{24,8},{28,12},{1,17},{... | collective-permute-start | bytes 122888 | tf_op jit(solution)/shard_map/ppermute | solution.py:391
  17.5 4.9 %collective-permute-start.2 = (s16[32,640]{1,0:T(8,128)(2,1)S(1)}, s16[32,640]{1,0:T(8,128)(2,1)S(1)}, u32[]{:S(2)}, u32[]{:S(2)}) collective-permute-start(s16[32,640]{1,0:T(8,128)(2,1)S(1)} %sum_terms.1.refs_0_), channel_id=1, source_target_pairs={{0,8},{4,12},{8,0},{12,4},{16,24},{20,28},{24,16},{28,20},{1,9},{5... | collective-permute-start | bytes 122888 | tf_op jit(solution)/shard_map/ppermute | solution.py:391
  22.5 5.5 %collective-permute-start.3 = (s16[128,640]{1,0:T(8,128)(2,1)S(1)}, s16[128,640]{1,0:T(8,128)(2,1)S(1)}, u32[]{:S(2)}, u32[]{:S(2)}) collective-permute-start(s16[128,640]{1,0:T(8,128)(2,1)S(1)} %join.1.refs_0_), channel_id=1, source_target_pairs={{0,4},{4,0},{8,12},{12,8},{16,20},{20,16},{24,28},{28,24},{1,5},{5... | collective-permute-start | bytes 491528 | tf_op jit(solution)/shard_map/ppermute | solution.py:391

commit v5 on v3

--- a/solution.py
+++ b/solution.py
@@ -433,8 +433,8 @@
         name="sum_terms",
     )(*[blocks] * parts)
     if strips == 8:
-        orders = ((0,), (1,), (6, 4, 2), (7, 5, 3))
-        from_z = [partner(sums, "strip", bits) for bits in (6, 4, 2)]
+        orders = ((0,), (1,), (4, 6, 2), (5, 7, 3))
+        from_z = [partner(sums, "strip", bits) for bits in (4, 6, 2)]
         *from_z, near = lax.optimization_barrier((*from_z, partner(sums, "strip", 1)))
         held = pl.pallas_call(
             join_kernel,

time: 32.5 us -> 32.4 us (level)
  no operation moved by 1% of the time
where the time goes in v5:
time: 32.4 us; the launch traced here: 32.1 us
  blocking collectives  10.5 us (32%)
  Pallas kernels  9.02 us (28%)
  starting transfers between devices  7.28 us (22%)
  waiting for transfers between devices  4.68 us (14%)
  between operations  0.67 us (2%)
    all_gather x1, blocking collectives, local(): blocks = lax.all_gather(terms, 'cells', axis=0, tiled=True)  10.5 us
    ppermute x5, starting transfers between devices, partner(): lax.ppermute(values, axis, [(n, n ^ bits) for n in range(lax.axis_size(ax...  7.28 us
    pallas_call x1, Pallas kernels, local(): pl.pallas_call(functools.partial(field_kernel, (depth, tiles, parts, stri...  4.84 us
    ppermute x5, waiting for transfers between devices, partner(): lax.ppermute(values, axis, [(n, n ^ bits) for n in range(lax.axis_size(ax...  4.68 us
    pallas_call x1, Pallas kernels, local(): pl.pallas_call(functools.partial(splat_kernel, tiles, parts), out_shape=j...  2.63 us
    pallas_call x1, Pallas kernels, local(): pl.pallas_call(functools.partial(tables_kernel, (depth, tiles, parts, car...  1.44 us
  transfers between devices with their start and end apart: 5, of which 2 were waited for; matrix products, arithmetic and copies ran while one was open for 0% of the time, Pallas kernels for 4%

profile of v5, /device:TPU:0, one launch (start us, length us, event | category | flops | bytes accessed | tf_op | source)
XLA Modules:
  0.0 32.1 jit_solution(11240383250889290085)
XLA Ops:
  0.6 2.6 %splat.1 = s16[160,640]{1,0:T(8,128)(2,1)} custom-call(s32[32,128]{1,0:T(8,128)} %bitcast.4, s32[32,128]{1,0:T(8,128)} %bitcast.6, f32[2,4096]{1,0:T(2,128)} %fracs_ref.1, f32[32,128]{1,0:T(8,128)} %bitcast.9, f32[640,128]{1,0:T(8,128)} %bitcast.8, s32[4,640]{1,0:T(4,128)} %cap_in.1, f32[4,640]{1,0:T(4,128)} %block_in.1), custom_call_target="tpu_custom_call" | custom-call | tf_op jit(solution)/shard_map/splat/pallas_call | solution.py:411
  3.3 10.5 %all_gather.3.refs_0_.refs_1_.refs_2_.refs_3_.codes_ref = s16[640,640]{1,0:T(8,128)(2,1)S(1)} all-gather(s16[160,640]{1,0:T(8,128)(2,1)} %splat.1), channel_id=1, replica_groups=mesh['strip'=8,'cells'=4] {'cells'}, dimensions={0}, use_global_device_ids=true | all-gather | bytes 1024000 | tf_op jit(solution)/shard_map/all_gather | solution.py:420
  13.7 0.0 copy-start
  13.7 0.0 copy-start.1
  13.7 0.0 copy-start.2
  13.7 0.0 copy-start.3
  13.7 0.1 sum_terms.1.refs_0_
  13.9 2.7 %collective-permute-start = (s16[32,640]{1,0:T(8,128)(2,1)S(1)}, s16[32,640]{1,0:T(8,128)(2,1)S(1)}, u32[]{:S(2)}, u32[]{:S(2)}) collective-permute-start(s16[32,640]{1,0:T(8,128)(2,1)S(1)} %sum_terms.1.refs_0_), channel_id=1, source_target_pairs={{0,16},{4,20},{8,24},{12,28},{16,0},{20,4},{24,8},{28,12},{1,17},{... | collective-permute-start | bytes 122888 | tf_op jit(solution)/shard_map/ppermute | solution.py:391
  16.5 1.3 %collective-permute-start.1 = (s16[32,640]{1,0:T(8,128)(2,1)S(1)}, s16[32,640]{1,0:T(8,128)(2,1)S(1)}, u32[]{:S(2)}, u32[]{:S(2)}) collective-permute-start(s16[32,640]{1,0:T(8,128)(2,1)S(1)} %sum_terms.1.refs_0_), channel_id=1, source_target_pairs={{0,24},{4,28},{8,16},{12,20},{16,8},{20,12},{24,0},{28,4},{1,25},{... | collective-permute-start | bytes 122888 | tf_op jit(solution)/shard_map/ppermute | solution.py:391
  17.9 0.2 collective-permute-start.2
  18.1 1.5 %collective-permute-start.3 = (s16[32,640]{1,0:T(8,128)(2,1)S(1)}, s16[32,640]{1,0:T(8,128)(2,1)S(1)}, u32[]{:S(2)}, u32[]{:S(2)}) collective-permute-start(s16[32,640]{1,0:T(8,128)(2,1)S(1)} %sum_terms.1.refs_0_), channel_id=1, source_target_pairs={{0,4},{4,0},{8,12},{12,8},{16,20},{20,16},{24,28},{28,24},{1,5},{5... | collective-permute-start | bytes 122888 | tf_op jit(solution)/shard_map/ppermute | solution.py:391
  19.6 0.0 collective-permute-done.refs_0_
  19.6 2.7 %collective-permute-done.1.refs_1_ = s16[32,640]{1,0:T(8,128)(2,1)S(1)} collective-permute-done((s16[32,640]{1,0:T(8,128)(2,1)S(1)}, s16[32,640]{1,0:T(8,128)(2,1)S(1)}, u32[]{:S(2)}, u32[]{:S(2)}) %collective-permute-start.1) | collective-permute-done | bytes 40992 | tf_op jit(solution)/shard_map/ppermute | solution.py:391
  22.3 0.0 collective-permute-done.2.refs_2_
  22.3 0.0 collective-permute-done.3.refs_1_
  22.3 1.6 %collective-permute-start.4 = (s16[96,640]{1,0:T(8,128)(2,1)S(1)}, s16[96,640]{1,0:T(8,128)(2,1)S(1)}, u32[]{:S(2)}, u32[]{:S(2)}) collective-permute-start(s16[96,640]{1,0:T(8,128)(2,1)S(1)} %join.1.refs_2_), channel_id=1, source_target_pairs={{0,4},{4,0},{8,12},{12,8},{16,20},{20,16},{24,28},{28,24},{1,5},{5... | collective-permute-start | bytes 368648 | tf_op jit(solution)/shard_map/ppermute | solution.py:391
  23.9 0.0 copy-done
  23.9 0.0 copy-done.1
  23.9 0.0 copy-done.2
  23.9 1.4 %tables.1 = (bf16[20,128,256]{2,1,0:T(8,128)(2,1)S(1)}, bf16[256,4096]{1,0:T(8,128)(2,1)S(1)}, f32[72,4096]{1,0:T(8,128)S(1)}) custom-call(s16[640,640]{1,0:T(8,128)(2,1)S(1)} %all_gather.3.refs_0_.refs_1_.refs_2_.refs_3_.codes_ref, s32[32,128]{1,0:T(8,128)S(1)} %bitcast.5, s32[32,128]{1,0:T(8,128)S(1)} %bitcast.7, f32[2,4096]{1,0:T(2,128)S(1)} %copy-done), custom_call_target="tpu_custom_call" | custom-call | flops 1048576 | bytes 2097152 | tf_op jit(solution)/shard_map/tables/pallas_call | solution.py:451
  25.4 1.9 %collective-permute-done.4.refs_3_ = s16[96,640]{1,0:T(8,128)(2,1)S(1)} collective-permute-done((s16[96,640]{1,0:T(8,128)(2,1)S(1)}, s16[96,640]{1,0:T(8,128)(2,1)S(1)}, u32[]{:S(2)}, u32[]{:S(2)}) %collective-permute-start.4) | collective-permute-done | bytes 122912 | tf_op jit(solution)/shard_map/ppermute | solution.py:391
  27.3 0.0 copy-done.3
  27.3 4.8 %field.1 = (f32[4,640]{1,0:T(4,128)}, f32[2,4096]{1,0:T(2,128)}) custom-call(bf16[20,128,256]{2,1,0:T(8,128)(2,1)S(1)} %get-tuple-element.15.pairs, bf16[256,4096]{1,0:T(8,128)(2,1)S(1)} %get-tuple-element.16.look_ref, f32[72,4096]{1,0:T(8,128)S(1)} %get-tuple-element.17.share_ref, f32[1,32,32]{2,1,0:T(8,128)S(1)} %copy-done.3, ...), custom_call_target="tpu_custom_call" | custom-call | tf_op jit(solution)/shard_map/field/pallas_call | solution.py:465
  (1 shorter events, 0.0 us)
Async XLA Ops:
  13.7 10.2 %copy-start = (f32[2,4096]{1,0:T(2,128)S(1)}, f32[2,4096]{1,0:T(2,128)}, u32[]{:S(2)}) copy-start(f32[2,4096]{1,0:T(2,128)} %fracs_ref.1) | copy-start | bytes 98308
  13.7 10.2 %copy-start.1 = (s32[4096]{0:T(1024)S(1)}, s32[4096]{0:T(1024)}, u32[]{:S(2)}) copy-start(s32[4096]{0:T(1024)} %param.8) | copy-start | bytes 49156
  13.7 10.2 %copy-start.2 = (s32[4096]{0:T(1024)S(1)}, s32[4096]{0:T(1024)}, u32[]{:S(2)}) copy-start(s32[4096]{0:T(1024)} %param.9) | copy-start | bytes 49156
  13.7 13.6 %copy-start.3 = (f32[1,32,32]{2,1,0:T(8,128)S(1)}, f32[1,32,32]{2,1,0:T(8,128)}, u32[]{:S(2)}) copy-start(f32[1,32,32]{2,1,0:T(8,128)} %col_blocks_ref.1) | copy-start | bytes 12292
  13.9 5.7 %collective-permute-start = (s16[32,640]{1,0:T(8,128)(2,1)S(1)}, s16[32,640]{1,0:T(8,128)(2,1)S(1)}, u32[]{:S(2)}, u32[]{:S(2)}) collective-permute-start(s16[32,640]{1,0:T(8,128)(2,1)S(1)} %sum_terms.1.refs_0_), channel_id=1, source_target_pairs={{0,16},{4,20},{8,24},{12,28},{16,0},{20,4},{24,8},{28,12},{1,17},{... | collective-permute-start | bytes 122888 | tf_op jit(solution)/shard_map/ppermute | solution.py:391
  16.5 5.8 %collective-permute-start.1 = (s16[32,640]{1,0:T(8,128)(2,1)S(1)}, s16[32,640]{1,0:T(8,128)(2,1)S(1)}, u32[]{:S(2)}, u32[]{:S(2)}) collective-permute-start(s16[32,640]{1,0:T(8,128)(2,1)S(1)} %sum_terms.1.refs_0_), channel_id=1, source_target_pairs={{0,24},{4,28},{8,16},{12,20},{16,8},{20,12},{24,0},{28,4},{1,25},{... | collective-permute-start | bytes 122888 | tf_op jit(solution)/shard_map/ppermute | solution.py:391
  17.9 4.5 %collective-permute-start.2 = (s16[32,640]{1,0:T(8,128)(2,1)S(1)}, s16[32,640]{1,0:T(8,128)(2,1)S(1)}, u32[]{:S(2)}, u32[]{:S(2)}) collective-permute-start(s16[32,640]{1,0:T(8,128)(2,1)S(1)} %sum_terms.1.refs_0_), channel_id=1, source_target_pairs={{0,8},{4,12},{8,0},{12,4},{16,24},{20,28},{24,16},{28,20},{1,9},{5... | collective-permute-start | bytes 122888 | tf_op jit(solution)/shard_map/ppermute | solution.py:391
  18.1 4.2 %collective-permute-start.3 = (s16[32,640]{1,0:T(8,128)(2,1)S(1)}, s16[32,640]{1,0:T(8,128)(2,1)S(1)}, u32[]{:S(2)}, u32[]{:S(2)}) collective-permute-start(s16[32,640]{1,0:T(8,128)(2,1)S(1)} %sum_terms.1.refs_0_), channel_id=1, source_target_pairs={{0,4},{4,0},{8,12},{12,8},{16,20},{20,16},{24,28},{28,24},{1,5},{5... | collective-permute-start | bytes 122888 | tf_op jit(solution)/shard_map/ppermute | solution.py:391
  22.3 4.9 %collective-permute-start.4 = (s16[96,640]{1,0:T(8,128)(2,1)S(1)}, s16[96,640]{1,0:T(8,128)(2,1)S(1)}, u32[]{:S(2)}, u32[]{:S(2)}) collective-permute-start(s16[96,640]{1,0:T(8,128)(2,1)S(1)} %join.1.refs_2_), channel_id=1, source_target_pairs={{0,4},{4,0},{8,12},{12,8},{16,20},{20,16},{24,28},{28,24},{1,5},{5... | collective-permute-start | bytes 368648 | tf_op jit(solution)/shard_map/ppermute | solution.py:391

commit v6 on v5

--- a/solution.py
+++ b/solution.py
@@ -16,7 +16,7 @@
 floor_level = 0.5
 block_low, block_span = -0.002, 0.152
 weight_low, weight_span = 0.5, 3.5
-term_low, term_octaves = -20.0, 34.0
+term_low, term_octaves = -24.0, 40.0
 code_top = 65535.0
 code_half = 32768.0
 log_two = 0.6931471805599453

time: 32.4 us -> 32.4 us (level)
  no operation moved by 1% of the time
where the time goes in v6:
time: 32.4 us; the launch traced here: 32.1 us
  blocking collectives  10.5 us (32%)
  Pallas kernels  9.02 us (28%)
  starting transfers between devices  7.28 us (22%)
  waiting for transfers between devices  4.68 us (14%)
  between operations  0.67 us (2%)
    all_gather x1, blocking collectives, local(): blocks = lax.all_gather(terms, 'cells', axis=0, tiled=True)  10.5 us
    ppermute x5, starting transfers between devices, partner(): lax.ppermute(values, axis, [(n, n ^ bits) for n in range(lax.axis_size(ax...  7.28 us
    pallas_call x1, Pallas kernels, local(): pl.pallas_call(functools.partial(field_kernel, (depth, tiles, parts, stri...  4.84 us
    ppermute x5, waiting for transfers between devices, partner(): lax.ppermute(values, axis, [(n, n ^ bits) for n in range(lax.axis_size(ax...  4.68 us
    pallas_call x1, Pallas kernels, local(): pl.pallas_call(functools.partial(splat_kernel, tiles, parts), out_shape=j...  2.63 us
    pallas_call x1, Pallas kernels, local(): pl.pallas_call(functools.partial(tables_kernel, (depth, tiles, parts, car...  1.44 us
  transfers between devices with their start and end apart: 5, of which 2 were waited for; matrix products, arithmetic and copies ran while one was open for 0% of the time, Pallas kernels for 4%

profile of v6, /device:TPU:0, one launch (start us, length us, event | category | flops | bytes accessed | tf_op | source)
XLA Modules:
  0.0 32.1 jit_solution(11093138653211149899)
XLA Ops:
  0.6 2.6 %splat.1 = s16[160,640]{1,0:T(8,128)(2,1)} custom-call(s32[32,128]{1,0:T(8,128)} %bitcast.4, s32[32,128]{1,0:T(8,128)} %bitcast.6, f32[2,4096]{1,0:T(2,128)} %fracs_ref.1, f32[32,128]{1,0:T(8,128)} %bitcast.9, f32[640,128]{1,0:T(8,128)} %bitcast.8, s32[4,640]{1,0:T(4,128)} %cap_in.1, f32[4,640]{1,0:T(4,128)} %block_in.1), custom_call_target="tpu_custom_call" | custom-call | tf_op jit(solution)/shard_map/splat/pallas_call | solution.py:411
  3.3 10.5 %all_gather.3.refs_0_.refs_1_.refs_2_.refs_3_.codes_ref = s16[640,640]{1,0:T(8,128)(2,1)S(1)} all-gather(s16[160,640]{1,0:T(8,128)(2,1)} %splat.1), channel_id=1, replica_groups=mesh['strip'=8,'cells'=4] {'cells'}, dimensions={0}, use_global_device_ids=true | all-gather | bytes 1024000 | tf_op jit(solution)/shard_map/all_gather | solution.py:420
  13.7 0.0 copy-start
  13.7 0.0 copy-start.1
  13.7 0.0 copy-start.2
  13.7 0.0 copy-start.3
  13.7 0.1 sum_terms.1.refs_0_
  13.9 2.7 %collective-permute-start = (s16[32,640]{1,0:T(8,128)(2,1)S(1)}, s16[32,640]{1,0:T(8,128)(2,1)S(1)}, u32[]{:S(2)}, u32[]{:S(2)}) collective-permute-start(s16[32,640]{1,0:T(8,128)(2,1)S(1)} %sum_terms.1.refs_0_), channel_id=1, source_target_pairs={{0,16},{4,20},{8,24},{12,28},{16,0},{20,4},{24,8},{28,12},{1,17},{... | collective-permute-start | bytes 122888 | tf_op jit(solution)/shard_map/ppermute | solution.py:391
  16.5 1.3 %collective-permute-start.1 = (s16[32,640]{1,0:T(8,128)(2,1)S(1)}, s16[32,640]{1,0:T(8,128)(2,1)S(1)}, u32[]{:S(2)}, u32[]{:S(2)}) collective-permute-start(s16[32,640]{1,0:T(8,128)(2,1)S(1)} %sum_terms.1.refs_0_), channel_id=1, source_target_pairs={{0,24},{4,28},{8,16},{12,20},{16,8},{20,12},{24,0},{28,4},{1,25},{... | collective-permute-start | bytes 122888 | tf_op jit(solution)/shard_map/ppermute | solution.py:391
  17.9 0.2 collective-permute-start.2
  18.1 1.5 %collective-permute-start.3 = (s16[32,640]{1,0:T(8,128)(2,1)S(1)}, s16[32,640]{1,0:T(8,128)(2,1)S(1)}, u32[]{:S(2)}, u32[]{:S(2)}) collective-permute-start(s16[32,640]{1,0:T(8,128)(2,1)S(1)} %sum_terms.1.refs_0_), channel_id=1, source_target_pairs={{0,4},{4,0},{8,12},{12,8},{16,20},{20,16},{24,28},{28,24},{1,5},{5... | collective-permute-start | bytes 122888 | tf_op jit(solution)/shard_map/ppermute | solution.py:391
  19.6 0.0 collective-permute-done.refs_0_
  19.6 2.7 %collective-permute-done.1.refs_1_ = s16[32,640]{1,0:T(8,128)(2,1)S(1)} collective-permute-done((s16[32,640]{1,0:T(8,128)(2,1)S(1)}, s16[32,640]{1,0:T(8,128)(2,1)S(1)}, u32[]{:S(2)}, u32[]{:S(2)}) %collective-permute-start.1) | collective-permute-done | bytes 40992 | tf_op jit(solution)/shard_map/ppermute | solution.py:391
  22.3 0.0 collective-permute-done.2.refs_2_
  22.3 0.0 collective-permute-done.3.refs_1_
  22.3 1.6 %collective-permute-start.4 = (s16[96,640]{1,0:T(8,128)(2,1)S(1)}, s16[96,640]{1,0:T(8,128)(2,1)S(1)}, u32[]{:S(2)}, u32[]{:S(2)}) collective-permute-start(s16[96,640]{1,0:T(8,128)(2,1)S(1)} %join.1.refs_2_), channel_id=1, source_target_pairs={{0,4},{4,0},{8,12},{12,8},{16,20},{20,16},{24,28},{28,24},{1,5},{5... | collective-permute-start | bytes 368648 | tf_op jit(solution)/shard_map/ppermute | solution.py:391
  23.9 0.0 copy-done
  23.9 0.0 copy-done.1
  23.9 0.0 copy-done.2
  23.9 1.4 %tables.1 = (bf16[20,128,256]{2,1,0:T(8,128)(2,1)S(1)}, bf16[256,4096]{1,0:T(8,128)(2,1)S(1)}, f32[72,4096]{1,0:T(8,128)S(1)}) custom-call(s16[640,640]{1,0:T(8,128)(2,1)S(1)} %all_gather.3.refs_0_.refs_1_.refs_2_.refs_3_.codes_ref, s32[32,128]{1,0:T(8,128)S(1)} %bitcast.5, s32[32,128]{1,0:T(8,128)S(1)} %bitcast.7, f32[2,4096]{1,0:T(2,128)S(1)} %copy-done), custom_call_target="tpu_custom_call" | custom-call | flops 1048576 | bytes 2097152 | tf_op jit(solution)/shard_map/tables/pallas_call | solution.py:451
  25.4 1.9 %collective-permute-done.4.refs_3_ = s16[96,640]{1,0:T(8,128)(2,1)S(1)} collective-permute-done((s16[96,640]{1,0:T(8,128)(2,1)S(1)}, s16[96,640]{1,0:T(8,128)(2,1)S(1)}, u32[]{:S(2)}, u32[]{:S(2)}) %collective-permute-start.4) | collective-permute-done | bytes 122912 | tf_op jit(solution)/shard_map/ppermute | solution.py:391
  27.3 0.0 copy-done.3
  27.3 4.8 %field.1 = (f32[4,640]{1,0:T(4,128)}, f32[2,4096]{1,0:T(2,128)}) custom-call(bf16[20,128,256]{2,1,0:T(8,128)(2,1)S(1)} %get-tuple-element.15.pairs, bf16[256,4096]{1,0:T(8,128)(2,1)S(1)} %get-tuple-element.16.look_ref, f32[72,4096]{1,0:T(8,128)S(1)} %get-tuple-element.17.share_ref, f32[1,32,32]{2,1,0:T(8,128)S(1)} %copy-done.3, ...), custom_call_target="tpu_custom_call" | custom-call | tf_op jit(solution)/shard_map/field/pallas_call | solution.py:465
  (1 shorter events, 0.0 us)
Async XLA Ops:
  13.7 10.2 %copy-start = (f32[2,4096]{1,0:T(2,128)S(1)}, f32[2,4096]{1,0:T(2,128)}, u32[]{:S(2)}) copy-start(f32[2,4096]{1,0:T(2,128)} %fracs_ref.1) | copy-start | bytes 98308
  13.7 10.2 %copy-start.1 = (s32[4096]{0:T(1024)S(1)}, s32[4096]{0:T(1024)}, u32[]{:S(2)}) copy-start(s32[4096]{0:T(1024)} %param.8) | copy-start | bytes 49156
  13.7 10.2 %copy-start.2 = (s32[4096]{0:T(1024)S(1)}, s32[4096]{0:T(1024)}, u32[]{:S(2)}) copy-start(s32[4096]{0:T(1024)} %param.9) | copy-start | bytes 49156
  13.7 13.6 %copy-start.3 = (f32[1,32,32]{2,1,0:T(8,128)S(1)}, f32[1,32,32]{2,1,0:T(8,128)}, u32[]{:S(2)}) copy-start(f32[1,32,32]{2,1,0:T(8,128)} %col_blocks_ref.1) | copy-start | bytes 12292
  13.9 5.7 %collective-permute-start = (s16[32,640]{1,0:T(8,128)(2,1)S(1)}, s16[32,640]{1,0:T(8,128)(2,1)S(1)}, u32[]{:S(2)}, u32[]{:S(2)}) collective-permute-start(s16[32,640]{1,0:T(8,128)(2,1)S(1)} %sum_terms.1.refs_0_), channel_id=1, source_target_pairs={{0,16},{4,20},{8,24},{12,28},{16,0},{20,4},{24,8},{28,12},{1,17},{... | collective-permute-start | bytes 122888 | tf_op jit(solution)/shard_map/ppermute | solution.py:391
  16.5 5.8 %collective-permute-start.1 = (s16[32,640]{1,0:T(8,128)(2,1)S(1)}, s16[32,640]{1,0:T(8,128)(2,1)S(1)}, u32[]{:S(2)}, u32[]{:S(2)}) collective-permute-start(s16[32,640]{1,0:T(8,128)(2,1)S(1)} %sum_terms.1.refs_0_), channel_id=1, source_target_pairs={{0,24},{4,28},{8,16},{12,20},{16,8},{20,12},{24,0},{28,4},{1,25},{... | collective-permute-start | bytes 122888 | tf_op jit(solution)/shard_map/ppermute | solution.py:391
  17.9 4.5 %collective-permute-start.2 = (s16[32,640]{1,0:T(8,128)(2,1)S(1)}, s16[32,640]{1,0:T(8,128)(2,1)S(1)}, u32[]{:S(2)}, u32[]{:S(2)}) collective-permute-start(s16[32,640]{1,0:T(8,128)(2,1)S(1)} %sum_terms.1.refs_0_), channel_id=1, source_target_pairs={{0,8},{4,12},{8,0},{12,4},{16,24},{20,28},{24,16},{28,20},{1,9},{5... | collective-permute-start | bytes 122888 | tf_op jit(solution)/shard_map/ppermute | solution.py:391
  18.1 4.2 %collective-permute-start.3 = (s16[32,640]{1,0:T(8,128)(2,1)S(1)}, s16[32,640]{1,0:T(8,128)(2,1)S(1)}, u32[]{:S(2)}, u32[]{:S(2)}) collective-permute-start(s16[32,640]{1,0:T(8,128)(2,1)S(1)} %sum_terms.1.refs_0_), channel_id=1, source_target_pairs={{0,4},{4,0},{8,12},{12,8},{16,20},{20,16},{24,28},{28,24},{1,5},{5... | collective-permute-start | bytes 122888 | tf_op jit(solution)/shard_map/ppermute | solution.py:391
  22.3 4.9 %collective-permute-start.4 = (s16[96,640]{1,0:T(8,128)(2,1)S(1)}, s16[96,640]{1,0:T(8,128)(2,1)S(1)}, u32[]{:S(2)}, u32[]{:S(2)}) collective-permute-start(s16[96,640]{1,0:T(8,128)(2,1)S(1)} %join.1.refs_2_), channel_id=1, source_target_pairs={{0,4},{4,0},{8,12},{12,8},{16,20},{20,16},{24,28},{28,24},{1,5},{5... | collective-permute-start | bytes 368648 | tf_op jit(solution)/shard_map/ppermute | solution.py:391

commit v7 on v6

--- a/solution.py
+++ b/solution.py
@@ -154,7 +154,7 @@
         return 2.0 * mine - left - right
 
 
-def delayed(count, first, second, delay=2):
+def delayed(count, first, second, delay=5):
     waiting, results = [], []
     for t in range(count + delay):
         if t < count:

time: 32.4 us -> 32.4 us (level)
  no operation moved by 1% of the time
where the time goes in v7:
time: 32.4 us; the launch traced here: 32.1 us
  blocking collectives  10.5 us (32%)
  Pallas kernels  9.02 us (28%)
  starting transfers between devices  7.28 us (22%)
  waiting for transfers between devices  4.68 us (14%)
  between operations  0.67 us (2%)
    all_gather x1, blocking collectives, local(): blocks = lax.all_gather(terms, 'cells', axis=0, tiled=True)  10.5 us
    ppermute x5, starting transfers between devices, partner(): lax.ppermute(values, axis, [(n, n ^ bits) for n in range(lax.axis_size(ax...  7.28 us
    pallas_call x1, Pallas kernels, local(): pl.pallas_call(functools.partial(field_kernel, (depth, tiles, parts, stri...  4.84 us
    ppermute x5, waiting for transfers between devices, partner(): lax.ppermute(values, axis, [(n, n ^ bits) for n in range(lax.axis_size(ax...  4.68 us
    pallas_call x1, Pallas kernels, local(): pl.pallas_call(functools.partial(splat_kernel, tiles, parts), out_shape=j...  2.63 us
    pallas_call x1, Pallas kernels, local(): pl.pallas_call(functools.partial(tables_kernel, (depth, tiles, parts, car...  1.44 us
  transfers between devices with their start and end apart: 5, of which 2 were waited for; matrix products, arithmetic and copies ran while one was open for 0% of the time, Pallas kernels for 4%

profile of v7, /device:TPU:0, one launch (start us, length us, event | category | flops | bytes accessed | tf_op | source)
XLA Modules:
  0.0 32.1 jit_solution(11093138653211149899)
XLA Ops:
  0.6 2.6 %splat.1 = s16[160,640]{1,0:T(8,128)(2,1)} custom-call(s32[32,128]{1,0:T(8,128)} %bitcast.4, s32[32,128]{1,0:T(8,128)} %bitcast.6, f32[2,4096]{1,0:T(2,128)} %fracs_ref.1, f32[32,128]{1,0:T(8,128)} %bitcast.9, f32[640,128]{1,0:T(8,128)} %bitcast.8, s32[4,640]{1,0:T(4,128)} %cap_in.1, f32[4,640]{1,0:T(4,128)} %block_in.1), custom_call_target="tpu_custom_call" | custom-call | tf_op jit(solution)/shard_map/splat/pallas_call | solution.py:411
  3.3 10.5 %all_gather.3.refs_0_.refs_1_.refs_2_.refs_3_.codes_ref = s16[640,640]{1,0:T(8,128)(2,1)S(1)} all-gather(s16[160,640]{1,0:T(8,128)(2,1)} %splat.1), channel_id=1, replica_groups=mesh['strip'=8,'cells'=4] {'cells'}, dimensions={0}, use_global_device_ids=true | all-gather | bytes 1024000 | tf_op jit(solution)/shard_map/all_gather | solution.py:420
  13.7 0.0 copy-start
  13.7 0.0 copy-start.1
  13.7 0.0 copy-start.2
  13.7 0.0 copy-start.3
  13.7 0.1 sum_terms.1.refs_0_
  13.9 2.7 %collective-permute-start = (s16[32,640]{1,0:T(8,128)(2,1)S(1)}, s16[32,640]{1,0:T(8,128)(2,1)S(1)}, u32[]{:S(2)}, u32[]{:S(2)}) collective-permute-start(s16[32,640]{1,0:T(8,128)(2,1)S(1)} %sum_terms.1.refs_0_), channel_id=1, source_target_pairs={{0,16},{4,20},{8,24},{12,28},{16,0},{20,4},{24,8},{28,12},{1,17},{... | collective-permute-start | bytes 122888 | tf_op jit(solution)/shard_map/ppermute | solution.py:391
  16.5 1.3 %collective-permute-start.1 = (s16[32,640]{1,0:T(8,128)(2,1)S(1)}, s16[32,640]{1,0:T(8,128)(2,1)S(1)}, u32[]{:S(2)}, u32[]{:S(2)}) collective-permute-start(s16[32,640]{1,0:T(8,128)(2,1)S(1)} %sum_terms.1.refs_0_), channel_id=1, source_target_pairs={{0,24},{4,28},{8,16},{12,20},{16,8},{20,12},{24,0},{28,4},{1,25},{... | collective-permute-start | bytes 122888 | tf_op jit(solution)/shard_map/ppermute | solution.py:391
  17.9 0.2 collective-permute-start.2
  18.1 1.5 %collective-permute-start.3 = (s16[32,640]{1,0:T(8,128)(2,1)S(1)}, s16[32,640]{1,0:T(8,128)(2,1)S(1)}, u32[]{:S(2)}, u32[]{:S(2)}) collective-permute-start(s16[32,640]{1,0:T(8,128)(2,1)S(1)} %sum_terms.1.refs_0_), channel_id=1, source_target_pairs={{0,4},{4,0},{8,12},{12,8},{16,20},{20,16},{24,28},{28,24},{1,5},{5... | collective-permute-start | bytes 122888 | tf_op jit(solution)/shard_map/ppermute | solution.py:391
  19.6 0.0 collective-permute-done.refs_0_
  19.6 2.7 %collective-permute-done.1.refs_1_ = s16[32,640]{1,0:T(8,128)(2,1)S(1)} collective-permute-done((s16[32,640]{1,0:T(8,128)(2,1)S(1)}, s16[32,640]{1,0:T(8,128)(2,1)S(1)}, u32[]{:S(2)}, u32[]{:S(2)}) %collective-permute-start.1) | collective-permute-done | bytes 40992 | tf_op jit(solution)/shard_map/ppermute | solution.py:391
  22.3 0.0 collective-permute-done.2.refs_2_
  22.3 0.0 collective-permute-done.3.refs_1_
  22.3 1.6 %collective-permute-start.4 = (s16[96,640]{1,0:T(8,128)(2,1)S(1)}, s16[96,640]{1,0:T(8,128)(2,1)S(1)}, u32[]{:S(2)}, u32[]{:S(2)}) collective-permute-start(s16[96,640]{1,0:T(8,128)(2,1)S(1)} %join.1.refs_2_), channel_id=1, source_target_pairs={{0,4},{4,0},{8,12},{12,8},{16,20},{20,16},{24,28},{28,24},{1,5},{5... | collective-permute-start | bytes 368648 | tf_op jit(solution)/shard_map/ppermute | solution.py:391
  23.9 0.0 copy-done
  23.9 0.0 copy-done.1
  23.9 0.0 copy-done.2
  23.9 1.4 %tables.1 = (bf16[20,128,256]{2,1,0:T(8,128)(2,1)S(1)}, bf16[256,4096]{1,0:T(8,128)(2,1)S(1)}, f32[72,4096]{1,0:T(8,128)S(1)}) custom-call(s16[640,640]{1,0:T(8,128)(2,1)S(1)} %all_gather.3.refs_0_.refs_1_.refs_2_.refs_3_.codes_ref, s32[32,128]{1,0:T(8,128)S(1)} %bitcast.5, s32[32,128]{1,0:T(8,128)S(1)} %bitcast.7, f32[2,4096]{1,0:T(2,128)S(1)} %copy-done), custom_call_target="tpu_custom_call" | custom-call | flops 1048576 | bytes 2097152 | tf_op jit(solution)/shard_map/tables/pallas_call | solution.py:451
  25.4 1.9 %collective-permute-done.4.refs_3_ = s16[96,640]{1,0:T(8,128)(2,1)S(1)} collective-permute-done((s16[96,640]{1,0:T(8,128)(2,1)S(1)}, s16[96,640]{1,0:T(8,128)(2,1)S(1)}, u32[]{:S(2)}, u32[]{:S(2)}) %collective-permute-start.4) | collective-permute-done | bytes 122912 | tf_op jit(solution)/shard_map/ppermute | solution.py:391
  27.3 0.0 copy-done.3
  27.3 4.8 %field.1 = (f32[4,640]{1,0:T(4,128)}, f32[2,4096]{1,0:T(2,128)}) custom-call(bf16[20,128,256]{2,1,0:T(8,128)(2,1)S(1)} %get-tuple-element.15.pairs, bf16[256,4096]{1,0:T(8,128)(2,1)S(1)} %get-tuple-element.16.look_ref, f32[72,4096]{1,0:T(8,128)S(1)} %get-tuple-element.17.share_ref, f32[1,32,32]{2,1,0:T(8,128)S(1)} %copy-done.3, ...), custom_call_target="tpu_custom_call" | custom-call | tf_op jit(solution)/shard_map/field/pallas_call | solution.py:465
  (1 shorter events, 0.0 us)
Async XLA Ops:
  13.7 10.2 %copy-start = (f32[2,4096]{1,0:T(2,128)S(1)}, f32[2,4096]{1,0:T(2,128)}, u32[]{:S(2)}) copy-start(f32[2,4096]{1,0:T(2,128)} %fracs_ref.1) | copy-start | bytes 98308
  13.7 10.2 %copy-start.1 = (s32[4096]{0:T(1024)S(1)}, s32[4096]{0:T(1024)}, u32[]{:S(2)}) copy-start(s32[4096]{0:T(1024)} %param.8) | copy-start | bytes 49156
  13.7 10.2 %copy-start.2 = (s32[4096]{0:T(1024)S(1)}, s32[4096]{0:T(1024)}, u32[]{:S(2)}) copy-start(s32[4096]{0:T(1024)} %param.9) | copy-start | bytes 49156
  13.7 13.6 %copy-start.3 = (f32[1,32,32]{2,1,0:T(8,128)S(1)}, f32[1,32,32]{2,1,0:T(8,128)}, u32[]{:S(2)}) copy-start(f32[1,32,32]{2,1,0:T(8,128)} %col_blocks_ref.1) | copy-start | bytes 12292
  13.9 5.7 %collective-permute-start = (s16[32,640]{1,0:T(8,128)(2,1)S(1)}, s16[32,640]{1,0:T(8,128)(2,1)S(1)}, u32[]{:S(2)}, u32[]{:S(2)}) collective-permute-start(s16[32,640]{1,0:T(8,128)(2,1)S(1)} %sum_terms.1.refs_0_), channel_id=1, source_target_pairs={{0,16},{4,20},{8,24},{12,28},{16,0},{20,4},{24,8},{28,12},{1,17},{... | collective-permute-start | bytes 122888 | tf_op jit(solution)/shard_map/ppermute | solution.py:391
  16.5 5.8 %collective-permute-start.1 = (s16[32,640]{1,0:T(8,128)(2,1)S(1)}, s16[32,640]{1,0:T(8,128)(2,1)S(1)}, u32[]{:S(2)}, u32[]{:S(2)}) collective-permute-start(s16[32,640]{1,0:T(8,128)(2,1)S(1)} %sum_terms.1.refs_0_), channel_id=1, source_target_pairs={{0,24},{4,28},{8,16},{12,20},{16,8},{20,12},{24,0},{28,4},{1,25},{... | collective-permute-start | bytes 122888 | tf_op jit(solution)/shard_map/ppermute | solution.py:391
  17.9 4.5 %collective-permute-start.2 = (s16[32,640]{1,0:T(8,128)(2,1)S(1)}, s16[32,640]{1,0:T(8,128)(2,1)S(1)}, u32[]{:S(2)}, u32[]{:S(2)}) collective-permute-start(s16[32,640]{1,0:T(8,128)(2,1)S(1)} %sum_terms.1.refs_0_), channel_id=1, source_target_pairs={{0,8},{4,12},{8,0},{12,4},{16,24},{20,28},{24,16},{28,20},{1,9},{5... | collective-permute-start | bytes 122888 | tf_op jit(solution)/shard_map/ppermute | solution.py:391
  18.1 4.2 %collective-permute-start.3 = (s16[32,640]{1,0:T(8,128)(2,1)S(1)}, s16[32,640]{1,0:T(8,128)(2,1)S(1)}, u32[]{:S(2)}, u32[]{:S(2)}) collective-permute-start(s16[32,640]{1,0:T(8,128)(2,1)S(1)} %sum_terms.1.refs_0_), channel_id=1, source_target_pairs={{0,4},{4,0},{8,12},{12,8},{16,20},{20,16},{24,28},{28,24},{1,5},{5... | collective-permute-start | bytes 122888 | tf_op jit(solution)/shard_map/ppermute | solution.py:391
  22.3 4.9 %collective-permute-start.4 = (s16[96,640]{1,0:T(8,128)(2,1)S(1)}, s16[96,640]{1,0:T(8,128)(2,1)S(1)}, u32[]{:S(2)}, u32[]{:S(2)}) collective-permute-start(s16[96,640]{1,0:T(8,128)(2,1)S(1)} %join.1.refs_2_), channel_id=1, source_target_pairs={{0,4},{4,0},{8,12},{12,8},{16,20},{20,16},{24,28},{28,24},{1,5},{5... | collective-permute-start | bytes 368648 | tf_op jit(solution)/shard_map/ppermute | solution.py:391

commit v8 on v6

--- a/solution.py
+++ b/solution.py
@@ -280,7 +280,7 @@
 
     col_blocks = [jnp.concatenate(halves(col_blocks_ref[k]), 0) for k in range(col_blocks_ref.shape[0])]
     inner = pl.ds(8, height)
-    lanes_at_once = 2 * LANES if chunks == 1 and width % (2 * LANES) == 0 else LANES
+    lanes_at_once = 4 * LANES if chunks == 1 and width % (4 * LANES) == 0 else LANES
     at_once = width // lanes_at_once if chunks == 1 else 1
 
     def cuts_of(g):

time: 32.4 us -> 32.4 us (level)
  no operation moved by 1% of the time
where the time goes in v8:
time: 32.4 us; the launch traced here: 32.1 us
  blocking collectives  10.5 us (32%)
  Pallas kernels  9.01 us (28%)
  starting transfers between devices  7.28 us (22%)
  waiting for transfers between devices  4.68 us (14%)
  between operations  0.67 us (2%)
    all_gather x1, blocking collectives, local(): blocks = lax.all_gather(terms, 'cells', axis=0, tiled=True)  10.5 us
    ppermute x5, starting transfers between devices, partner(): lax.ppermute(values, axis, [(n, n ^ bits) for n in range(lax.axis_size(ax...  7.28 us
    pallas_call x1, Pallas kernels, local(): pl.pallas_call(functools.partial(field_kernel, (depth, tiles, parts, stri...  4.83 us
    ppermute x5, waiting for transfers between devices, partner(): lax.ppermute(values, axis, [(n, n ^ bits) for n in range(lax.axis_size(ax...  4.68 us
    pallas_call x1, Pallas kernels, local(): pl.pallas_call(functools.partial(splat_kernel, tiles, parts), out_shape=j...  2.63 us
    pallas_call x1, Pallas kernels, local(): pl.pallas_call(functools.partial(tables_kernel, (depth, tiles, parts, car...  1.44 us
  transfers between devices with their start and end apart: 5, of which 2 were waited for; matrix products, arithmetic and copies ran while one was open for 0% of the time, Pallas kernels for 4%

profile of v8, /device:TPU:0, one launch (start us, length us, event | category | flops | bytes accessed | tf_op | source)
XLA Modules:
  0.0 32.1 jit_solution(5860248373104392040)
XLA Ops:
  0.6 2.6 %splat.1 = s16[160,640]{1,0:T(8,128)(2,1)} custom-call(s32[32,128]{1,0:T(8,128)} %bitcast.4, s32[32,128]{1,0:T(8,128)} %bitcast.6, f32[2,4096]{1,0:T(2,128)} %fracs_ref.1, f32[32,128]{1,0:T(8,128)} %bitcast.9, f32[640,128]{1,0:T(8,128)} %bitcast.8, s32[4,640]{1,0:T(4,128)} %cap_in.1, f32[4,640]{1,0:T(4,128)} %block_in.1), custom_call_target="tpu_custom_call" | custom-call | tf_op jit(solution)/shard_map/splat/pallas_call | solution.py:411
  3.3 10.5 %all_gather.3.refs_0_.refs_1_.refs_2_.refs_3_.codes_ref = s16[640,640]{1,0:T(8,128)(2,1)S(1)} all-gather(s16[160,640]{1,0:T(8,128)(2,1)} %splat.1), channel_id=1, replica_groups=mesh['strip'=8,'cells'=4] {'cells'}, dimensions={0}, use_global_device_ids=true | all-gather | bytes 1024000 | tf_op jit(solution)/shard_map/all_gather | solution.py:420
  13.7 0.0 copy-start
  13.7 0.0 copy-start.1
  13.7 0.0 copy-start.2
  13.7 0.0 copy-start.3
  13.7 0.1 sum_terms.1.refs_0_
  13.9 2.7 %collective-permute-start = (s16[32,640]{1,0:T(8,128)(2,1)S(1)}, s16[32,640]{1,0:T(8,128)(2,1)S(1)}, u32[]{:S(2)}, u32[]{:S(2)}) collective-permute-start(s16[32,640]{1,0:T(8,128)(2,1)S(1)} %sum_terms.1.refs_0_), channel_id=1, source_target_pairs={{0,16},{4,20},{8,24},{12,28},{16,0},{20,4},{24,8},{28,12},{1,17},{... | collective-permute-start | bytes 122888 | tf_op jit(solution)/shard_map/ppermute | solution.py:391
  16.5 1.3 %collective-permute-start.1 = (s16[32,640]{1,0:T(8,128)(2,1)S(1)}, s16[32,640]{1,0:T(8,128)(2,1)S(1)}, u32[]{:S(2)}, u32[]{:S(2)}) collective-permute-start(s16[32,640]{1,0:T(8,128)(2,1)S(1)} %sum_terms.1.refs_0_), channel_id=1, source_target_pairs={{0,24},{4,28},{8,16},{12,20},{16,8},{20,12},{24,0},{28,4},{1,25},{... | collective-permute-start | bytes 122888 | tf_op jit(solution)/shard_map/ppermute | solution.py:391
  17.9 0.2 collective-permute-start.2
  18.1 1.5 %collective-permute-start.3 = (s16[32,640]{1,0:T(8,128)(2,1)S(1)}, s16[32,640]{1,0:T(8,128)(2,1)S(1)}, u32[]{:S(2)}, u32[]{:S(2)}) collective-permute-start(s16[32,640]{1,0:T(8,128)(2,1)S(1)} %sum_terms.1.refs_0_), channel_id=1, source_target_pairs={{0,4},{4,0},{8,12},{12,8},{16,20},{20,16},{24,28},{28,24},{1,5},{5... | collective-permute-start | bytes 122888 | tf_op jit(solution)/shard_map/ppermute | solution.py:391
  19.6 0.0 collective-permute-done.refs_0_
  19.6 2.7 %collective-permute-done.1.refs_1_ = s16[32,640]{1,0:T(8,128)(2,1)S(1)} collective-permute-done((s16[32,640]{1,0:T(8,128)(2,1)S(1)}, s16[32,640]{1,0:T(8,128)(2,1)S(1)}, u32[]{:S(2)}, u32[]{:S(2)}) %collective-permute-start.1) | collective-permute-done | bytes 40992 | tf_op jit(solution)/shard_map/ppermute | solution.py:391
  22.3 0.0 collective-permute-done.2.refs_2_
  22.3 0.0 collective-permute-done.3.refs_1_
  22.3 1.6 %collective-permute-start.4 = (s16[96,640]{1,0:T(8,128)(2,1)S(1)}, s16[96,640]{1,0:T(8,128)(2,1)S(1)}, u32[]{:S(2)}, u32[]{:S(2)}) collective-permute-start(s16[96,640]{1,0:T(8,128)(2,1)S(1)} %join.1.refs_2_), channel_id=1, source_target_pairs={{0,4},{4,0},{8,12},{12,8},{16,20},{20,16},{24,28},{28,24},{1,5},{5... | collective-permute-start | bytes 368648 | tf_op jit(solution)/shard_map/ppermute | solution.py:391
  23.9 0.0 copy-done
  23.9 0.0 copy-done.1
  23.9 0.0 copy-done.2
  23.9 1.4 %tables.1 = (bf16[20,128,256]{2,1,0:T(8,128)(2,1)S(1)}, bf16[256,4096]{1,0:T(8,128)(2,1)S(1)}, f32[72,4096]{1,0:T(8,128)S(1)}) custom-call(s16[640,640]{1,0:T(8,128)(2,1)S(1)} %all_gather.3.refs_0_.refs_1_.refs_2_.refs_3_.codes_ref, s32[32,128]{1,0:T(8,128)S(1)} %bitcast.5, s32[32,128]{1,0:T(8,128)S(1)} %bitcast.7, f32[2,4096]{1,0:T(2,128)S(1)} %copy-done), custom_call_target="tpu_custom_call" | custom-call | flops 1048576 | bytes 2097152 | tf_op jit(solution)/shard_map/tables/pallas_call | solution.py:451
  25.4 1.9 %collective-permute-done.4.refs_3_ = s16[96,640]{1,0:T(8,128)(2,1)S(1)} collective-permute-done((s16[96,640]{1,0:T(8,128)(2,1)S(1)}, s16[96,640]{1,0:T(8,128)(2,1)S(1)}, u32[]{:S(2)}, u32[]{:S(2)}) %collective-permute-start.4) | collective-permute-done | bytes 122912 | tf_op jit(solution)/shard_map/ppermute | solution.py:391
  27.3 0.0 copy-done.3
  27.3 4.8 %field.1 = (f32[4,640]{1,0:T(4,128)}, f32[2,4096]{1,0:T(2,128)}) custom-call(bf16[20,128,256]{2,1,0:T(8,128)(2,1)S(1)} %get-tuple-element.15.pairs, bf16[256,4096]{1,0:T(8,128)(2,1)S(1)} %get-tuple-element.16.look_ref, f32[72,4096]{1,0:T(8,128)S(1)} %get-tuple-element.17.share_ref, f32[1,32,32]{2,1,0:T(8,128)S(1)} %copy-done.3, ...), custom_call_target="tpu_custom_call" | custom-call | tf_op jit(solution)/shard_map/field/pallas_call | solution.py:465
  (1 shorter events, 0.0 us)
Async XLA Ops:
  13.7 10.2 %copy-start = (f32[2,4096]{1,0:T(2,128)S(1)}, f32[2,4096]{1,0:T(2,128)}, u32[]{:S(2)}) copy-start(f32[2,4096]{1,0:T(2,128)} %fracs_ref.1) | copy-start | bytes 98308
  13.7 10.2 %copy-start.1 = (s32[4096]{0:T(1024)S(1)}, s32[4096]{0:T(1024)}, u32[]{:S(2)}) copy-start(s32[4096]{0:T(1024)} %param.8) | copy-start | bytes 49156
  13.7 10.2 %copy-start.2 = (s32[4096]{0:T(1024)S(1)}, s32[4096]{0:T(1024)}, u32[]{:S(2)}) copy-start(s32[4096]{0:T(1024)} %param.9) | copy-start | bytes 49156
  13.7 13.6 %copy-start.3 = (f32[1,32,32]{2,1,0:T(8,128)S(1)}, f32[1,32,32]{2,1,0:T(8,128)}, u32[]{:S(2)}) copy-start(f32[1,32,32]{2,1,0:T(8,128)} %col_blocks_ref.1) | copy-start | bytes 12292
  13.9 5.7 %collective-permute-start = (s16[32,640]{1,0:T(8,128)(2,1)S(1)}, s16[32,640]{1,0:T(8,128)(2,1)S(1)}, u32[]{:S(2)}, u32[]{:S(2)}) collective-permute-start(s16[32,640]{1,0:T(8,128)(2,1)S(1)} %sum_terms.1.refs_0_), channel_id=1, source_target_pairs={{0,16},{4,20},{8,24},{12,28},{16,0},{20,4},{24,8},{28,12},{1,17},{... | collective-permute-start | bytes 122888 | tf_op jit(solution)/shard_map/ppermute | solution.py:391
  16.5 5.8 %collective-permute-start.1 = (s16[32,640]{1,0:T(8,128)(2,1)S(1)}, s16[32,640]{1,0:T(8,128)(2,1)S(1)}, u32[]{:S(2)}, u32[]{:S(2)}) collective-permute-start(s16[32,640]{1,0:T(8,128)(2,1)S(1)} %sum_terms.1.refs_0_), channel_id=1, source_target_pairs={{0,24},{4,28},{8,16},{12,20},{16,8},{20,12},{24,0},{28,4},{1,25},{... | collective-permute-start | bytes 122888 | tf_op jit(solution)/shard_map/ppermute | solution.py:391
  17.9 4.5 %collective-permute-start.2 = (s16[32,640]{1,0:T(8,128)(2,1)S(1)}, s16[32,640]{1,0:T(8,128)(2,1)S(1)}, u32[]{:S(2)}, u32[]{:S(2)}) collective-permute-start(s16[32,640]{1,0:T(8,128)(2,1)S(1)} %sum_terms.1.refs_0_), channel_id=1, source_target_pairs={{0,8},{4,12},{8,0},{12,4},{16,24},{20,28},{24,16},{28,20},{1,9},{5... | collective-permute-start | bytes 122888 | tf_op jit(solution)/shard_map/ppermute | solution.py:391
  18.1 4.2 %collective-permute-start.3 = (s16[32,640]{1,0:T(8,128)(2,1)S(1)}, s16[32,640]{1,0:T(8,128)(2,1)S(1)}, u32[]{:S(2)}, u32[]{:S(2)}) collective-permute-start(s16[32,640]{1,0:T(8,128)(2,1)S(1)} %sum_terms.1.refs_0_), channel_id=1, source_target_pairs={{0,4},{4,0},{8,12},{12,8},{16,20},{20,16},{24,28},{28,24},{1,5},{5... | collective-permute-start | bytes 122888 | tf_op jit(solution)/shard_map/ppermute | solution.py:391
  22.3 4.9 %collective-permute-start.4 = (s16[96,640]{1,0:T(8,128)(2,1)S(1)}, s16[96,640]{1,0:T(8,128)(2,1)S(1)}, u32[]{:S(2)}, u32[]{:S(2)}) collective-permute-start(s16[96,640]{1,0:T(8,128)(2,1)S(1)} %join.1.refs_2_), channel_id=1, source_target_pairs={{0,4},{4,0},{8,12},{12,8},{16,20},{20,16},{24,28},{28,24},{1,5},{5... | collective-permute-start | bytes 368648 | tf_op jit(solution)/shard_map/ppermute | solution.py:391

commit v9 on v6

--- a/solution.py
+++ b/solution.py
@@ -378,7 +378,7 @@
 
     table = jnp.concatenate([table_of(velocity_y), table_of(velocity_x)], 0).astype(bf16)
     pins = share_ref.shape[1]
-    at_once = 2 * LANES if pins % (2 * LANES) == 0 else LANES
+    at_once = 4 * LANES if pins % (4 * LANES) == 0 else LANES
     for j in range(0, pins, at_once):
         cut = slice(j, j + at_once)
         sampled = jnp.dot(table, look_ref[:, cut], preferred_element_type=f32)

time: 32.4 us -> 32.4 us (level)
  no operation moved by 1% of the time
where the time goes in v9:
time: 32.4 us; the launch traced here: 32.1 us
  blocking collectives  10.5 us (32%)
  Pallas kernels  9.02 us (28%)
  starting transfers between devices  7.28 us (22%)
  waiting for transfers between devices  4.68 us (14%)
  between operations  0.67 us (2%)
    all_gather x1, blocking collectives, local(): blocks = lax.all_gather(terms, 'cells', axis=0, tiled=True)  10.5 us
    ppermute x5, starting transfers between devices, partner(): lax.ppermute(values, axis, [(n, n ^ bits) for n in range(lax.axis_size(ax...  7.28 us
    pallas_call x1, Pallas kernels, local(): pl.pallas_call(functools.partial(field_kernel, (depth, tiles, parts, stri...  4.84 us
    ppermute x5, waiting for transfers between devices, partner(): lax.ppermute(values, axis, [(n, n ^ bits) for n in range(lax.axis_size(ax...  4.68 us
    pallas_call x1, Pallas kernels, local(): pl.pallas_call(functools.partial(splat_kernel, tiles, parts), out_shape=j...  2.63 us
    pallas_call x1, Pallas kernels, local(): pl.pallas_call(functools.partial(tables_kernel, (depth, tiles, parts, car...  1.44 us
  transfers between devices with their start and end apart: 5, of which 2 were waited for; matrix products, arithmetic and copies ran while one was open for 0% of the time, Pallas kernels for 4%

profile of v9, /device:TPU:0, one launch (start us, length us, event | category | flops | bytes accessed | tf_op | source)
XLA Modules:
  0.0 32.1 jit_solution(8357310945026610984)
XLA Ops:
  0.6 2.6 %splat.1 = s16[160,640]{1,0:T(8,128)(2,1)} custom-call(s32[32,128]{1,0:T(8,128)} %bitcast.4, s32[32,128]{1,0:T(8,128)} %bitcast.6, f32[2,4096]{1,0:T(2,128)} %fracs_ref.1, f32[32,128]{1,0:T(8,128)} %bitcast.9, f32[640,128]{1,0:T(8,128)} %bitcast.8, s32[4,640]{1,0:T(4,128)} %cap_in.1, f32[4,640]{1,0:T(4,128)} %block_in.1), custom_call_target="tpu_custom_call" | custom-call | tf_op jit(solution)/shard_map/splat/pallas_call | solution.py:411
  3.3 10.5 %all_gather.3.refs_0_.refs_1_.refs_2_.refs_3_.codes_ref = s16[640,640]{1,0:T(8,128)(2,1)S(1)} all-gather(s16[160,640]{1,0:T(8,128)(2,1)} %splat.1), channel_id=1, replica_groups=mesh['strip'=8,'cells'=4] {'cells'}, dimensions={0}, use_global_device_ids=true | all-gather | bytes 1024000 | tf_op jit(solution)/shard_map/all_gather | solution.py:420
  13.7 0.0 copy-start
  13.7 0.0 copy-start.1
  13.7 0.0 copy-start.2
  13.7 0.0 copy-start.3
  13.7 0.1 sum_terms.1.refs_0_
  13.9 2.7 %collective-permute-start = (s16[32,640]{1,0:T(8,128)(2,1)S(1)}, s16[32,640]{1,0:T(8,128)(2,1)S(1)}, u32[]{:S(2)}, u32[]{:S(2)}) collective-permute-start(s16[32,640]{1,0:T(8,128)(2,1)S(1)} %sum_terms.1.refs_0_), channel_id=1, source_target_pairs={{0,16},{4,20},{8,24},{12,28},{16,0},{20,4},{24,8},{28,12},{1,17},{... | collective-permute-start | bytes 122888 | tf_op jit(solution)/shard_map/ppermute | solution.py:391
  16.5 1.3 %collective-permute-start.1 = (s16[32,640]{1,0:T(8,128)(2,1)S(1)}, s16[32,640]{1,0:T(8,128)(2,1)S(1)}, u32[]{:S(2)}, u32[]{:S(2)}) collective-permute-start(s16[32,640]{1,0:T(8,128)(2,1)S(1)} %sum_terms.1.refs_0_), channel_id=1, source_target_pairs={{0,24},{4,28},{8,16},{12,20},{16,8},{20,12},{24,0},{28,4},{1,25},{... | collective-permute-start | bytes 122888 | tf_op jit(solution)/shard_map/ppermute | solution.py:391
  17.9 0.2 collective-permute-start.2
  18.1 1.5 %collective-permute-start.3 = (s16[32,640]{1,0:T(8,128)(2,1)S(1)}, s16[32,640]{1,0:T(8,128)(2,1)S(1)}, u32[]{:S(2)}, u32[]{:S(2)}) collective-permute-start(s16[32,640]{1,0:T(8,128)(2,1)S(1)} %sum_terms.1.refs_0_), channel_id=1, source_target_pairs={{0,4},{4,0},{8,12},{12,8},{16,20},{20,16},{24,28},{28,24},{1,5},{5... | collective-permute-start | bytes 122888 | tf_op jit(solution)/shard_map/ppermute | solution.py:391
  19.6 0.0 collective-permute-done.refs_0_
  19.6 2.7 %collective-permute-done.1.refs_1_ = s16[32,640]{1,0:T(8,128)(2,1)S(1)} collective-permute-done((s16[32,640]{1,0:T(8,128)(2,1)S(1)}, s16[32,640]{1,0:T(8,128)(2,1)S(1)}, u32[]{:S(2)}, u32[]{:S(2)}) %collective-permute-start.1) | collective-permute-done | bytes 40992 | tf_op jit(solution)/shard_map/ppermute | solution.py:391
  22.3 0.0 collective-permute-done.2.refs_2_
  22.3 0.0 collective-permute-done.3.refs_1_
  22.3 1.6 %collective-permute-start.4 = (s16[96,640]{1,0:T(8,128)(2,1)S(1)}, s16[96,640]{1,0:T(8,128)(2,1)S(1)}, u32[]{:S(2)}, u32[]{:S(2)}) collective-permute-start(s16[96,640]{1,0:T(8,128)(2,1)S(1)} %join.1.refs_2_), channel_id=1, source_target_pairs={{0,4},{4,0},{8,12},{12,8},{16,20},{20,16},{24,28},{28,24},{1,5},{5... | collective-permute-start | bytes 368648 | tf_op jit(solution)/shard_map/ppermute | solution.py:391
  23.9 0.0 copy-done
  23.9 0.0 copy-done.1
  23.9 0.0 copy-done.2
  23.9 1.4 %tables.1 = (bf16[20,128,256]{2,1,0:T(8,128)(2,1)S(1)}, bf16[256,4096]{1,0:T(8,128)(2,1)S(1)}, f32[72,4096]{1,0:T(8,128)S(1)}) custom-call(s16[640,640]{1,0:T(8,128)(2,1)S(1)} %all_gather.3.refs_0_.refs_1_.refs_2_.refs_3_.codes_ref, s32[32,128]{1,0:T(8,128)S(1)} %bitcast.5, s32[32,128]{1,0:T(8,128)S(1)} %bitcast.7, f32[2,4096]{1,0:T(2,128)S(1)} %copy-done), custom_call_target="tpu_custom_call" | custom-call | flops 1048576 | bytes 2097152 | tf_op jit(solution)/shard_map/tables/pallas_call | solution.py:451
  25.4 1.9 %collective-permute-done.4.refs_3_ = s16[96,640]{1,0:T(8,128)(2,1)S(1)} collective-permute-done((s16[96,640]{1,0:T(8,128)(2,1)S(1)}, s16[96,640]{1,0:T(8,128)(2,1)S(1)}, u32[]{:S(2)}, u32[]{:S(2)}) %collective-permute-start.4) | collective-permute-done | bytes 122912 | tf_op jit(solution)/shard_map/ppermute | solution.py:391
  27.3 0.0 copy-done.3
  27.3 4.8 %field.1 = (f32[4,640]{1,0:T(4,128)}, f32[2,4096]{1,0:T(2,128)}) custom-call(bf16[20,128,256]{2,1,0:T(8,128)(2,1)S(1)} %get-tuple-element.15.pairs, bf16[256,4096]{1,0:T(8,128)(2,1)S(1)} %get-tuple-element.16.look_ref, f32[72,4096]{1,0:T(8,128)S(1)} %get-tuple-element.17.share_ref, f32[1,32,32]{2,1,0:T(8,128)S(1)} %copy-done.3, ...), custom_call_target="tpu_custom_call" | custom-call | tf_op jit(solution)/shard_map/field/pallas_call | solution.py:465
  (1 shorter events, 0.0 us)
Async XLA Ops:
  13.7 10.2 %copy-start = (f32[2,4096]{1,0:T(2,128)S(1)}, f32[2,4096]{1,0:T(2,128)}, u32[]{:S(2)}) copy-start(f32[2,4096]{1,0:T(2,128)} %fracs_ref.1) | copy-start | bytes 98308
  13.7 10.2 %copy-start.1 = (s32[4096]{0:T(1024)S(1)}, s32[4096]{0:T(1024)}, u32[]{:S(2)}) copy-start(s32[4096]{0:T(1024)} %param.8) | copy-start | bytes 49156
  13.7 10.2 %copy-start.2 = (s32[4096]{0:T(1024)S(1)}, s32[4096]{0:T(1024)}, u32[]{:S(2)}) copy-start(s32[4096]{0:T(1024)} %param.9) | copy-start | bytes 49156
  13.7 13.6 %copy-start.3 = (f32[1,32,32]{2,1,0:T(8,128)S(1)}, f32[1,32,32]{2,1,0:T(8,128)}, u32[]{:S(2)}) copy-start(f32[1,32,32]{2,1,0:T(8,128)} %col_blocks_ref.1) | copy-start | bytes 12292
  13.9 5.7 %collective-permute-start = (s16[32,640]{1,0:T(8,128)(2,1)S(1)}, s16[32,640]{1,0:T(8,128)(2,1)S(1)}, u32[]{:S(2)}, u32[]{:S(2)}) collective-permute-start(s16[32,640]{1,0:T(8,128)(2,1)S(1)} %sum_terms.1.refs_0_), channel_id=1, source_target_pairs={{0,16},{4,20},{8,24},{12,28},{16,0},{20,4},{24,8},{28,12},{1,17},{... | collective-permute-start | bytes 122888 | tf_op jit(solution)/shard_map/ppermute | solution.py:391
  16.5 5.8 %collective-permute-start.1 = (s16[32,640]{1,0:T(8,128)(2,1)S(1)}, s16[32,640]{1,0:T(8,128)(2,1)S(1)}, u32[]{:S(2)}, u32[]{:S(2)}) collective-permute-start(s16[32,640]{1,0:T(8,128)(2,1)S(1)} %sum_terms.1.refs_0_), channel_id=1, source_target_pairs={{0,24},{4,28},{8,16},{12,20},{16,8},{20,12},{24,0},{28,4},{1,25},{... | collective-permute-start | bytes 122888 | tf_op jit(solution)/shard_map/ppermute | solution.py:391
  17.9 4.5 %collective-permute-start.2 = (s16[32,640]{1,0:T(8,128)(2,1)S(1)}, s16[32,640]{1,0:T(8,128)(2,1)S(1)}, u32[]{:S(2)}, u32[]{:S(2)}) collective-permute-start(s16[32,640]{1,0:T(8,128)(2,1)S(1)} %sum_terms.1.refs_0_), channel_id=1, source_target_pairs={{0,8},{4,12},{8,0},{12,4},{16,24},{20,28},{24,16},{28,20},{1,9},{5... | collective-permute-start | bytes 122888 | tf_op jit(solution)/shard_map/ppermute | solution.py:391
  18.1 4.2 %collective-permute-start.3 = (s16[32,640]{1,0:T(8,128)(2,1)S(1)}, s16[32,640]{1,0:T(8,128)(2,1)S(1)}, u32[]{:S(2)}, u32[]{:S(2)}) collective-permute-start(s16[32,640]{1,0:T(8,128)(2,1)S(1)} %sum_terms.1.refs_0_), channel_id=1, source_target_pairs={{0,4},{4,0},{8,12},{12,8},{16,20},{20,16},{24,28},{28,24},{1,5},{5... | collective-permute-start | bytes 122888 | tf_op jit(solution)/shard_map/ppermute | solution.py:391
  22.3 4.9 %collective-permute-start.4 = (s16[96,640]{1,0:T(8,128)(2,1)S(1)}, s16[96,640]{1,0:T(8,128)(2,1)S(1)}, u32[]{:S(2)}, u32[]{:S(2)}) collective-permute-start(s16[96,640]{1,0:T(8,128)(2,1)S(1)} %join.1.refs_2_), channel_id=1, source_target_pairs={{0,4},{4,0},{8,12},{12,8},{16,20},{20,16},{24,28},{28,24},{1,5},{5... | collective-permute-start | bytes 368648 | tf_op jit(solution)/shard_map/ppermute | solution.py:391
